TPU v7x, 512 devices: a whole 4x4x16 slice. The times are simulated.
512 devices in a mesh: pipe: 16 (over y_lo, x, core), ep: 32 (over y_hi, z).
Axes of the slice: x: 4, y: 4 (y_hi: 2, y_lo: 2; y = y_hi * 2 + y_lo), z: 16, core: 2. Of those that a mesh axis runs over, the one named last changes fastest.
Arguments:
- tokens: bfloat16 [4096, 7168], P('ep'), may hold values from -6 to 6
- norm_gain: float32 [7168], replicated, may hold values from 0.1 to 1.9
- router: bfloat16 [7168, 256], P('pipe'), may hold values from -0.0625 to 0.0625
- routes: int32 [4096, 8], P('ep'), may hold values from 0 to 255, all different within a row; in each aligned block of 128 rows (0 to 127, 128 to 255, ...) at most 8 rows name the same one
- w_gate_up: bfloat16 [32, 7168, 2048], P('ep', None, 'pipe'), may hold values from -0.0625 to 0.0625
- w_down: bfloat16 [32, 1024, 7168], P('ep', 'pipe'), may hold values from -0.25 to 0.25
Outputs:
- mixed: bfloat16 [4096, 7168], P('ep', 'pipe')
Inputs may be any that keep to these rules, and one draw needn't show every extreme that they name: `routes`: each row names 8 different experts. Among the rows of one index of ep (aligned blocks of 128 rows) no expert is named more than 8 times, a bound that some block reaches.
All inputs are finite; a program needn't handle non-finite values.
Results may differ from a plain program's by a relative error of at most 0.011.
Values may be sent and summed in bfloat16 or wider, within the bound.
A program may use at most 128 MiB of HBM per device.

v0:
```python
import jax
import jax.numpy as jnp
from jax import lax
from jax.sharding import PartitionSpec as P


def shards(tokens, norm_gain, router, routes, w_gate_up, w_down):
    tok_dev, width = tokens.shape
    experts_all = router.shape[1]
    top_count = routes.shape[1]
    experts = lax.axis_size("ep")
    group_units = w_down.shape[1]
    capacity = max(2, 2 * tok_dev * top_count // experts_all)
    pipe_count = lax.axis_size("pipe")
    columns = width // pipe_count
    pipe_index = lax.axis_index("pipe")
    values = tokens.astype(jnp.float32)
    scale = lax.rsqrt(jnp.mean(values * values, axis=1, keepdims=True) + 1e-06)
    normed = (values * scale * norm_gain).astype(jnp.bfloat16)
    own_block = lax.dynamic_slice_in_dim(normed, pipe_index * columns, columns, 1)
    partial_logits = jnp.dot(own_block, router, preferred_element_type=jnp.float32)
    logits = lax.psum(partial_logits.astype(jnp.bfloat16), "pipe").astype(jnp.float32)
    affinity = jax.nn.sigmoid(logits)
    picked = jnp.take_along_axis(affinity, routes, axis=1)
    route_weight = 2.5 * picked / jnp.sum(picked, axis=1, keepdims=True)
    flat_routes = routes.reshape(-1)
    onehot = (flat_routes[:, None] == jnp.arange(experts, dtype=jnp.int32)[None, :]).astype(
        jnp.int32
    )
    slots = jnp.sum(onehot * (jnp.cumsum(onehot, axis=0) - 1), axis=1)
    sentinel = experts * capacity
    position = jnp.where(flat_routes < experts, flat_routes * capacity + slots, sentinel)
    position_grid = position.reshape(tok_dev, top_count)
    matches = position_grid[:, :, None] == jnp.arange(sentinel, dtype=jnp.int32)[None, None, :]
    placing = jnp.any(matches, axis=1).astype(jnp.bfloat16)
    combining = jnp.sum(jnp.where(matches, route_weight[:, :, None], 0.0), axis=1)
    outgoing = jnp.einsum("ts,td->sd", placing, normed, preferred_element_type=jnp.float32)
    outgoing = outgoing.astype(jnp.bfloat16).reshape(experts, capacity, width)
    received = lax.all_to_all(outgoing, "ep", split_axis=0, concat_axis=0, tiled=True)
    sources = received.shape[0]
    count = received.shape[1]
    inputs = received.reshape(sources * count, width)
    both = jnp.dot(inputs, w_gate_up[0], preferred_element_type=jnp.float32)
    gate = both[:, :group_units]
    upper = both[:, group_units:]
    hidden = (jax.nn.silu(gate) * upper).astype(jnp.bfloat16)
    partial_value = jnp.dot(hidden, w_down[0], preferred_element_type=jnp.float32).astype(
        jnp.bfloat16
    )
    returned = lax.all_to_all(
        partial_value.reshape(sources, count, width), "ep", split_axis=0, concat_axis=0, tiled=True
    )
    row_width = returned.shape[2]
    flat_returned = returned.reshape(sentinel, row_width).astype(jnp.float32)
    weighted = jnp.dot(
        combining,
        flat_returned,
        preferred_element_type=jnp.float32,
        precision=lax.Precision.HIGHEST,
    )
    residual = lax.dynamic_slice_in_dim(values, pipe_index * columns, columns, 1)
    summed = lax.psum_scatter(
        weighted.astype(jnp.bfloat16), "pipe", scatter_dimension=1, tiled=True
    ).astype(jnp.float32)
    return (residual + summed).astype(jnp.bfloat16)


def solution(mesh):
    placed = (
        P("ep", None),
        P(),
        P("pipe", None),
        P("ep", None),
        P("ep", None, "pipe"),
        P("ep", "pipe", None),
    )
    return jax.shard_map(
        shards, mesh=mesh, in_specs=placed, out_specs=P("ep", "pipe"), check_vma=False
    )
```

profile of v0, /device:TPU:1, one launch (start us, length us, event | category | flops | bytes accessed | tf_op | source)
XLA Modules:
  0.0 469.7 jit_solution(14956067516026472414)
XLA Ops:
  6.5 0.9 copy.39
  7.5 0.1 eq.42
  7.6 0.1 eq.38
  7.6 3.9 copy.38
  11.6 2.5 multiply_reduce_fusion
  14.1 9.0 %reduce-window.6 = s32[32,8,128]{2,1,0:T(8,128)S(1)} reduce-window(s32[32,8,128]{2,1,0:T(8,128)S(1)} %fusion.10, s32[]{:T(128)} %constant.17.clone.1), window={size=1x1x128 pad=0_0x0_0x127_0}, to_apply=%region_0.0 | reduce-window | flops 4161536 | bytes 262148 | tf_op jit(solution)/shard_map/reduce-window
  23.1 0.1 slice.18
  23.2 0.1 copy.41
  23.4 0.1 add_add_fusion
  23.7 0.1 copy.44
  23.8 0.4 fusion.6
  24.3 4.2 multiply_convert_fusion
  28.4 1.2 copy-done.1
  29.7 1.1 fusion.1
  30.8 184.8 %all_to_all.10 = bf16[32,8,7168]{2,1,0:T(8,128)(2,1)S(1)} all-to-all(bf16[32,8,7168]{2,1,0:T(8,128)(2,1)S(1)} %fusion.1), channel_id=1, replica_groups=mesh['pipe'=16,'ep'=32] {'ep'}, dimensions={0} | all-to-all | bytes 7340032 | tf_op jit(solution)/shard_map/all_to_all | solution.py:39
  215.6 1.3 fusion.3
  217.0 3.0 fusion
  220.0 6.4 %all-to-all-start.1 = ((bf16[32,8,7168]{2,1,0:T(8,128)(2,1)}), bf16[32,8,7168]{2,1,0:T(8,128)(2,1)}, u32[]{:S(2)}, u32[]{:S(2)}) async-start(bf16[32,8,7168]{2,1,0:T(8,128)(2,1)} %fusion), calls=%async_computation.1 | async-start | bytes 7340032 | tf_op jit(solution)/shard_map/all_to_all | solution.py:50
  226.5 1.8 convolution_convert_fusion.3
  228.3 0.2 reduce-scatter.2.cloned.1.call-start
  228.5 0.1 copy.45
  228.6 0.1 reshape.76
  228.7 127.5 %all-reduce.2.cloned.1.call-done = bf16[128,256]{1,0:T(8,128)(2,1)} async-done(((bf16[128,256]{1,0:T(8,128)(2,1)}), bf16[128,256]{1,0:T(8,128)(2,1)}) %all-reduce.2.cloned.1.call-update) | async-done | bytes 65552 | tf_op jit(solution)/shard_map/psum | solution.py:22
  356.2 0.9 add_divide_fusion
  357.1 8.6 %gather_fusion = f32[1024]{0:T(1024)S(1)} fusion(f32[128,256]{1,0:T(8,128)S(1)} %add_divide_fusion, s32[1024]{0:T(1024)S(1)} %reshape.76), kind=kCustom, calls=%fused_computation | custom fusion | bytes 16384 | tf_op jit(solution)/shard_map/jit(take_along_axis)/gather | solution.py:24
  365.9 0.1 copy.47
  366.0 0.4 select_reduce_fusion
  366.4 22.6 %all-to-all-done.1 = bf16[32,8,7168]{2,1,0:T(8,128)(2,1)} async-done(((bf16[32,8,7168]{2,1,0:T(8,128)(2,1)}), bf16[32,8,7168]{2,1,0:T(8,128)(2,1)}, u32[]{:S(2)}, u32[]{:S(2)}) %all-to-all-start.1) | async-done | bytes 3670048 | tf_op jit(solution)/shard_map/all_to_all | solution.py:50
  389.0 7.3 %convolution_convert_fusion.2 = bf16[128,7168]{0,1:T(8,128)(2,1)} fusion(f32[128,256]{1,0:T(8,128)S(1)} %select_reduce_fusion, bf16[32,8,7168]{2,1,0:T(8,128)(2,1)} %all-to-all-done.1), kind=kOutput, calls=%fused_computation.5 | convolution fusion | flops 2819489792 | bytes 5636096 | tf_op jit(solution)/shard_map/dot_general | solution.py:55
  396.4 3.5 convert_element_type.37
  399.9 61.3 %reduce-scatter.2.cloned.1.call-done = bf16[128,448]{0,1:T(8,128)(2,1)} async-done(((bf16[128,7168]{0,1:T(8,128)(2,1)}), bf16[128,448]{0,1:T(8,128)(2,1)}) %reduce-scatter.2.cloned.1.call-update) | async-done | bytes 114704 | tf_op jit(solution)/shard_map/reduce_scatter | solution.py:62
  461.2 1.7 add_convert_fusion
  (28 shorter events, 0.6 us)
Async XLA Ops:
  6.5 209.1 %copy-start = (bf16[1,7168,128]{2,1,0:T(8,128)(2,1)S(1)}, bf16[1,7168,128]{2,1,0:T(8,128)(2,1)}, u32[]{:S(2)}) copy-start(bf16[1,7168,128]{2,1,0:T(8,128)(2,1)} %param.10) | copy-start | bytes 5505028
  6.5 17.2 %copy-start.4 = (s32[128,8]{0,1:T(8,128)S(1)}, s32[128,8]{0,1:T(8,128)}, u32[]{:S(2)}) copy-start(s32[128,8]{0,1:T(8,128)} %param.9) | copy-start | bytes 12292
  6.5 17.7 %copy-start.5 = (f32[7168]{0:T(1024)S(1)}, f32[7168]{0:T(1024)}, u32[]{:S(2)}) copy-start(f32[7168]{0:T(1024)} %param.7) | copy-start | bytes 86020
  28.4 1.3 copy-start.1
  215.6 1.3 copy-start.2
  220.0 6.5 %copy-start.3 = (bf16[448,256]{1,0:T(8,128)(2,1)S(1)}, bf16[448,256]{1,0:T(8,128)(2,1)}, u32[]{:S(2)}) copy-start(bf16[448,256]{1,0:T(8,128)(2,1)} %param.8) | copy-start | bytes 688132
  220.0 169.1 %all-to-all-start.1 = ((bf16[32,8,7168]{2,1,0:T(8,128)(2,1)}), bf16[32,8,7168]{2,1,0:T(8,128)(2,1)}, u32[]{:S(2)}, u32[]{:S(2)}) async-start(bf16[32,8,7168]{2,1,0:T(8,128)(2,1)} %fusion), calls=%async_computation.1 | async-start | bytes 7340032 | tf_op jit(solution)/shard_map/all_to_all | solution.py:50
  226.4 129.8 %all-reduce.2.cloned.1.call-start = ((), (), s32[]{:S(2)}) async-start(), calls=%async_computation.3 | async-start | bytes 131072 | tf_op jit(solution)/shard_map/psum | solution.py:22
  228.3 232.9 %reduce-scatter.2.cloned.1.call-start = ((), (), s32[]{:S(2)}) async-start(), calls=%async_computation.4 | async-start | bytes 1949696 | tf_op jit(solution)/shard_map/reduce_scatter | solution.py:62
Sparse Core Ops, SparseCore 0:
  230.2 126.0 all-reduce.1
  396.5 64.6 reduce-scatter.1
where the time goes:
time: 472 us; the launch traced here: 470 us
  waiting for transfers between devices  211 us (45%)
  blocking collectives  185 us (39%)
  other arithmetic  22.7 us (5%)
  local copies, waits for them, and re-layouts  15.8 us (3%)
  matrix products  14.6 us (3%)
  between operations  13.6 us (3%)
  starting transfers between devices  6.71 us (1%)
    all_to_all x1, blocking collectives, shards(): lax.all_to_all(outgoing, 'ep', split_axis=0, concat_axis=0, tiled=True)  185 us
    psum x1, waiting for transfers between devices, shards(): lax.psum(partial_logits.astype(jnp.bfloat16), 'pipe').astype(jnp.float32)  128 us
    reduce_scatter x1, waiting for transfers between devices, shards(): lax.psum_scatter(weighted.astype(jnp.bfloat16), 'pipe', scatter_dimension...  61.3 us
    all_to_all x1, waiting for transfers between devices, shards(): lax.all_to_all(partial_value.reshape(sources, count, width), 'ep', split_...  22.6 us
  transfers between devices with their start and end apart: 3, of which 3 were waited for; matrix products, arithmetic and copies ran while one was open for 3% of the time, Pallas kernels for 0%

commit v1 on v0

v1 whole, which is shorter than its diff:
```python
import functools

import jax
import jax.numpy as jnp
from jax import lax
from jax.experimental import pallas as pl
from jax.experimental.pallas import tpu as pltpu
from jax.sharding import PartitionSpec as P

CORES = 2
NX = 4
NY = 2
CHIPS = NX * NY
PIPE = CHIPS * CORES
NZ = 16
HALVES = 2
CAP = 8
LANES = 128
MESH = pl.DeviceIdType.MESH


def remote(src, dst, send, recv, pipe, ep):
    return pltpu.make_async_remote_copy(
        src_ref=src,
        dst_ref=dst,
        send_sem=send,
        recv_sem=recv,
        device_id=(pipe, ep),
        device_id_type=MESH,
    )


def one_hot(routes, first, count, width):
    lane = lax.broadcasted_iota(jnp.int32, (routes.shape[0], width), 1)
    expert = first + lane // count
    named = routes[:, 0:1] == expert
    for k in range(1, routes.shape[1]):
        named = named | (routes[:, k : k + 1] == expert)
    return jnp.where(named, 1.0, 0.0), lane


def slot_matrix(routes, first, width):
    named, lane = one_hot(routes, first, CAP, width)
    rows = routes.shape[0]
    above = lax.broadcasted_iota(jnp.int32, (rows, rows), 1) < lax.broadcasted_iota(
        jnp.int32, (rows, rows), 0
    )
    rank = jnp.dot(
        jnp.where(above, 1.0, 0.0).astype(jnp.bfloat16),
        named.astype(jnp.bfloat16),
        preferred_element_type=jnp.float32,
    )
    return jnp.where(rank == (lane % CAP).astype(jnp.float32), named, 0.0)


def kernel(
    tokens_hbm, gain_ref, router_hbm, routes_ref, gate_up_hbm, down_hbm, out_ref,
    tokens, router, gate_up, down,
    outbox, inbox, rows, part, pair_in, summed, sums_in, back_out, back_in,
    score_out, score_in, weight_out, weight_in,
    load_sem, near_sem, out_sem, gather_send, gather_recv, share_send, share_recv,
    pair_send, pair_recv, sum_send, sum_recv, back_sem, back_near,
    score_sem, weight_sem,
):
    pipe, ep = lax.axis_index("pipe"), lax.axis_index("ep")
    core, chip = lax.rem(pipe, CORES), lax.div(pipe, CORES)
    x, y = lax.rem(chip, NX), lax.div(chip, NX)
    z, side = lax.rem(ep, NZ), lax.div(ep, NZ)
    far_side = lax.rem(side + core, HALVES)
    partner = pipe + 1 - 2 * core
    tok, width = tokens.shape
    columns = width // CHIPS
    tiles = columns // LANES
    half = NZ * CAP
    own = columns // CORES

    loads = []
    for number, (src, dst) in enumerate(
        ((tokens_hbm, tokens), (router_hbm, router.at[pl.ds(core * own, own), :]),
         (gate_up_hbm.at[0], gate_up), (down_hbm.at[0], down))
    ):
        if number == 1:
            router[...] = jnp.zeros_like(router)
        loads.append(pltpu.make_async_copy(src, dst, load_sem.at[number]))
        loads[-1].start()

    barrier = pltpu.get_barrier_semaphore()

    def greet_pipe(i, _):
        pl.semaphore_signal(
            barrier, inc=1, device_id=(lax.rem(pipe + i, PIPE), ep), device_id_type=MESH
        )
        return 0

    lax.fori_loop(1, PIPE, greet_pipe, 0)

    def greet_ep(i, _):
        other = lax.rem(z + i, NZ)
        for k in range(CORES):
            pl.semaphore_signal(
                barrier, inc=1,
                device_id=(CORES * chip + k, lax.rem(side + k, HALVES) * NZ + other),
                device_id_type=MESH,
            )
        return 0

    lax.fori_loop(1, NZ, greet_ep, 0)
    pl.semaphore_signal(
        barrier, inc=1,
        device_id=(CORES * chip + 1, (1 - side) * NZ + z), device_id_type=MESH,
    )

    @pl.when(core == 1)
    def _():
        pl.semaphore_signal(barrier, inc=1, device_id=(partner, ep), device_id_type=MESH)

    routes = routes_ref[...]
    mine = slot_matrix(routes, lax.rem(core + side, HALVES) * NZ, half)
    placing = jnp.transpose(mine).astype(jnp.bfloat16)

    loads[0].wait()
    squares = jnp.zeros((tok, LANES), jnp.float32)
    for at in range(width // LANES):
        values = tokens[:, at * LANES : (at + 1) * LANES].astype(jnp.float32)
        squares += values * values
    scale = lax.rsqrt(jnp.sum(squares, axis=1, keepdims=True) / width + 1e-06)
    block = pl.ds(pl.multiple_of(chip * columns, LANES), columns)
    normed = (tokens[:, block].astype(jnp.float32) * scale * gain_ref[:, block]).astype(
        jnp.bfloat16
    )
    placed = jnp.dot(placing, normed, preferred_element_type=jnp.float32)
    pieces = [
        placed[:, at * LANES : (at + 1) * LANES].reshape(NZ, CAP, LANES)
        for at in range(tiles)
    ]
    pieces.append(jnp.zeros((NZ, CAP, LANES), jnp.float32))
    outbox[...] = jnp.concatenate(pieces, axis=1).astype(jnp.bfloat16)

    pl.semaphore_wait(barrier, PIPE - 1 + 2 * NZ - 1 + core)

    def dispatch(i, _):
        other = lax.rem(z + i, NZ)
        remote(
            outbox.at[other], inbox.at[z], out_sem.at[0], out_sem.at[1],
            pipe, far_side * NZ + other,
        ).start()
        return 0

    lax.fori_loop(1, NZ, dispatch, 0)
    near = remote(
        outbox.at[z], inbox.at[z], near_sem.at[0], near_sem.at[1], pipe, far_side * NZ + z
    )

    @pl.when(core == 1)
    def _():
        near.start()

    @pl.when(core == 0)
    def _():
        pltpu.make_async_copy(outbox.at[z], inbox.at[z], near_sem.at[1]).start()

    loads[1].wait()
    scores = jnp.dot(normed, router[...], preferred_element_type=jnp.float32)
    score_out[...] = scores.reshape(score_out.shape)
    score_in[pipe] = score_out[pipe]

    def send_scores(i, _):
        other = lax.rem(pipe + i, PIPE)
        remote(
            score_out.at[other], score_in.at[pipe], score_sem.at[0], score_sem.at[1], other, ep
        ).start()
        return 0

    lax.fori_loop(1, PIPE, send_scores, 0)

    most = pl.ds(0, NZ - 1)
    pltpu.make_async_copy(inbox.at[most], inbox.at[most], out_sem.at[1]).wait()
    pltpu.make_async_copy(inbox.at[0], inbox.at[0], near_sem.at[1]).wait()
    arrived = inbox[...].astype(jnp.float32)
    keep = pl.ds(pl.multiple_of(core * half, half), half)
    give = pl.ds(pl.multiple_of((1 - core) * half, half), half)
    for at in range(tiles):
        rows[chip, keep, at * LANES : (at + 1) * LANES] = (
            arrived[:, at * CAP : (at + 1) * CAP, :].reshape(half, LANES).astype(jnp.bfloat16)
        )

    def chip_at(ry, rx):
        return lax.rem(y + ry, NY) * NX + lax.rem(x + rx, NX)

    relative = [(ry, rx) for rx in (2, 1, 3, 0) for ry in (1, 0) if (ry, rx) != (0, 0)]
    mirror = {(ry, rx): ry * NX + (NX - rx) % NX for ry, rx in relative}

    def gather_to(ry, rx):
        return remote(
            rows.at[chip, keep, :], rows.at[chip, keep, :],
            gather_send.at[ry * NX + rx], gather_recv.at[mirror[ry, rx]],
            CORES * chip_at(ry, rx) + core, ep,
        )

    def share(ry, rx):
        which = chip_at(ry, rx)
        return remote(
            rows.at[which, keep, :], rows.at[which, keep, :],
            share_send.at[ry * NX + rx], share_recv.at[ry * NX + rx], partner, ep,
        )

    for ry, rx in relative:
        gather_to(ry, rx).start()
    share(0, 0).start()

    most_pipe = pl.ds(0, PIPE - 1)
    pltpu.make_async_copy(score_in.at[most_pipe], score_in.at[most_pipe], score_sem.at[1]).wait()
    affinity = jax.nn.sigmoid(jnp.sum(score_in[...], axis=0))
    group = weight_out.shape[0]
    own_routes = routes_ref[pl.ds(pl.multiple_of(pipe * group, group), group), :]
    chosen, _ = one_hot(own_routes, 0, 1, affinity.shape[1])
    fraction = 2.5 * affinity / jnp.sum(chosen * affinity, axis=1, keepdims=True)
    total_slots = HALVES * half
    spread_row = lax.broadcasted_iota(jnp.int32, (affinity.shape[1], total_slots), 0)
    spread_lane = lax.broadcasted_iota(jnp.int32, (affinity.shape[1], total_slots), 1)
    slot_expert = lax.rem(spread_lane // CAP + side * NZ, HALVES * NZ)
    weight_out[...] = jnp.dot(
        fraction, jnp.where(spread_row == slot_expert, 1.0, 0.0),
        preferred_element_type=jnp.float32, precision=lax.Precision.HIGHEST,
    )
    weight_in[pipe] = weight_out[...]

    def send_weights(i, _):
        other = lax.rem(pipe + i, PIPE)
        remote(weight_out, weight_in.at[pipe], weight_sem.at[0], weight_sem.at[1], other, ep).start()
        return 0

    lax.fori_loop(1, PIPE, send_weights, 0)

    loads[2].wait()

    def project(which):
        return jnp.dot(
            rows[which],
            gate_up[pl.ds(pl.multiple_of(which * columns, LANES), columns), :],
            preferred_element_type=jnp.float32,
        )

    order = [(1, 0), (0, 1), (0, 3), (1, 1), (1, 3), (0, 2), (1, 2)]
    share(0, 0).wait_recv()
    both = project(chip)
    for ry, rx in order:
        gather_to(ry, (NX - rx) % NX).wait_recv()
        share(ry, rx).start()
    for ry, rx in order:
        share(ry, rx).wait_recv()
        both += project(chip_at(ry, rx))
    units = down.shape[0]
    gate, upper = both[:, :units], both[:, units:]
    hidden = (gate / (1.0 + jnp.exp(-gate)) * upper).astype(jnp.bfloat16)

    loads[3].wait()

    def to_partner(ry, rx):
        which = chip_at(ry, rx)
        return remote(
            part.at[which, give, :], pair_in.at[which],
            pair_send.at[ry * NX + rx], pair_recv.at[ry * NX + rx], partner, ep,
        )

    def to_owner(ry, rx):
        return remote(
            summed.at[chip_at(ry, rx)], sums_in.at[mirror[ry, rx]],
            sum_send.at[ry * NX + rx], sum_recv.at[mirror[ry, rx]],
            CORES * chip_at(ry, rx) + core, ep,
        )

    outward = relative + [(0, 0)]
    for ry, rx in outward:
        which = chip_at(ry, rx)
        part[which] = jnp.dot(
            hidden, down[:, pl.ds(pl.multiple_of(which * columns, LANES), columns)],
            preferred_element_type=jnp.float32,
        ).astype(jnp.bfloat16)
        to_partner(ry, rx).start()
    for ry, rx in relative:
        which = chip_at(ry, rx)
        to_partner(ry, rx).wait_recv()
        summed[which] = (
            part[which, keep, :].astype(jnp.float32) + pair_in[which].astype(jnp.float32)
        ).astype(jnp.bfloat16)
        to_owner(ry, rx).start()
    to_partner(0, 0).wait_recv()
    result = part[chip, keep, :].astype(jnp.float32) + pair_in[chip].astype(jnp.float32)

    placed_all = slot_matrix(routes, 0, total_slots)
    first = pl.ds(0, half)
    slots_now = jnp.where(
        side == 0, placed_all,
        jnp.concatenate([placed_all[:, half:], placed_all[:, :half]], axis=1),
    )

    for ry, rx in order:
        to_owner(ry, (NX - rx) % NX).wait_recv()
        result += sums_in[ry * NX + rx].astype(jnp.float32)

    for j in range(CORES):
        pieces = []
        for at in range(4):
            low = j * own + at * LANES
            high = min(low + LANES, (j + 1) * own)
            piece = result[:, low:high]
            if high - low < LANES:
                piece = jnp.concatenate(
                    [piece, jnp.zeros((half, LANES - (high - low)), jnp.float32)], axis=1
                )
            pieces.append(piece.reshape(NZ, CAP, LANES))
        back_out[j] = jnp.concatenate(pieces, axis=1).astype(jnp.bfloat16)

    def go_back(i, _):
        other = lax.rem(z + i, NZ)
        for j in range(CORES):
            remote(
                back_out.at[j, other], back_in.at[core, z], back_sem.at[0], back_sem.at[1],
                CORES * chip + j, far_side * NZ + other,
            ).start()
        return 0

    lax.fori_loop(1, NZ, go_back, 0)
    back_one = remote(
        back_out.at[1, z], back_in.at[core, z], back_near.at[1], back_near.at[2 + core],
        CORES * chip + 1, far_side * NZ + z,
    )
    back_zero = remote(
        back_out.at[0, z], back_in.at[core, z], back_near.at[0], back_near.at[2 + core],
        CORES * chip, far_side * NZ + z,
    )
    back_one.start()

    @pl.when(core == 1)
    def _():
        back_zero.start()

    @pl.when(core == 0)
    def _():
        pltpu.make_async_copy(
            back_out.at[0, z], back_in.at[core, z], back_near.at[2 + core]
        ).start()

    pltpu.make_async_copy(
        weight_in.at[most_pipe], weight_in.at[most_pipe], weight_sem.at[1]
    ).wait()
    combining = slots_now * weight_in[...].reshape(tok, total_slots)
    chip_tokens = tokens[:, block].astype(jnp.float32)
    residual = jnp.where(core == 0, chip_tokens[:, :own], chip_tokens[:, own:])

    pltpu.make_async_copy(
        back_in.at[:, most], back_in.at[:, most], back_sem.at[1]
    ).wait()
    for k in range(HALVES):
        pltpu.make_async_copy(back_in.at[k, 0], back_in.at[k, 0], back_near.at[2 + k]).wait()
    returned = back_in[...].astype(jnp.float32)
    returned = jnp.concatenate(
        [
            returned[:, :, at * CAP : (at + 1) * CAP, :].reshape(total_slots, LANES)
            for at in range(4)
        ],
        axis=1,
    )
    mixed = jnp.dot(
        combining, returned, preferred_element_type=jnp.float32, precision=lax.Precision.HIGHEST
    )
    out_ref[...] = (residual + mixed[:, :own]).astype(jnp.bfloat16)

    pltpu.make_async_copy(outbox.at[most], outbox.at[most], out_sem.at[0]).wait()

    @pl.when(core == 1)
    def _():
        near.wait_send()
        back_zero.wait_send()

    back_one.wait_send()
    pltpu.make_async_copy(back_out.at[:, most], back_out.at[:, most], back_sem.at[0]).wait()
    pltpu.make_async_copy(
        score_out.at[most_pipe], score_out.at[most_pipe], score_sem.at[0]
    ).wait()
    pltpu.make_async_copy(
        weight_in.at[most_pipe], weight_in.at[most_pipe], weight_sem.at[0]
    ).wait()
    for ry, rx in relative:
        gather_to(ry, rx).wait_send()
        to_owner(ry, rx).wait_send()
    for ry, rx in outward:
        share(ry, rx).wait_send()
        to_partner(ry, rx).wait_send()


def shards(tokens, norm_gain, router, routes, w_gate_up, w_down):
    tok, width = tokens.shape
    columns = width // CHIPS
    half = NZ * CAP
    units = w_down.shape[1]
    experts = router.shape[1]
    group = tok // PIPE
    bf16, f32 = jnp.bfloat16, jnp.float32
    dma = pltpu.SemaphoreType.DMA
    anywhere = pl.BlockSpec(memory_space=pl.ANY)
    vmem = pl.BlockSpec(memory_space=pltpu.VMEM)
    return pl.pallas_call(
        kernel,
        out_shape=jax.ShapeDtypeStruct((tok, width // PIPE), bf16),
        in_specs=[anywhere, vmem, anywhere, vmem, anywhere, anywhere],
        out_specs=vmem,
        scratch_shapes=[
            pltpu.VMEM((tok, width), bf16),
            pltpu.VMEM((columns, experts), bf16),
            pltpu.VMEM((width, 2 * units), bf16),
            pltpu.VMEM((units, width), bf16),
            pltpu.VMEM((NZ, 64, LANES), bf16),
            pltpu.VMEM((NZ, 64, LANES), bf16),
            pltpu.VMEM((CHIPS, 2 * half, columns), bf16),
            pltpu.VMEM((CHIPS, 2 * half, columns), bf16),
            pltpu.VMEM((CHIPS, half, columns), bf16),
            pltpu.VMEM((CHIPS, half, columns), bf16),
            pltpu.VMEM((CHIPS, half, columns), bf16),
            pltpu.VMEM((CORES, NZ, 32, LANES), bf16),
            pltpu.VMEM((HALVES, NZ, 32, LANES), bf16),
            pltpu.VMEM((PIPE, group, experts), f32),
            pltpu.VMEM((PIPE, group, experts), f32),
            pltpu.VMEM((group, 2 * half), f32),
            pltpu.VMEM((PIPE, group, 2 * half), f32),
            dma((4,)), dma((2,)), dma((2,)),
            dma((CHIPS,)), dma((CHIPS,)), dma((CHIPS,)), dma((CHIPS,)),
            dma((CHIPS,)), dma((CHIPS,)), dma((CHIPS,)), dma((CHIPS,)),
            dma((2,)), dma((4,)), dma((2,)), dma((2,)),
        ],
        compiler_params=pltpu.CompilerParams(
            collective_id=0, has_side_effects=True, vmem_limit_bytes=56 * 1024 * 1024
        ),
        cost_estimate=pl.CostEstimate(
            flops=2_000_000_000, bytes_accessed=8_000_000, transcendentals=100_000
        ),
    )(tokens, norm_gain.reshape(1, width), router, routes, w_gate_up, w_down)


def solution(mesh):
    placed = (
        P("ep", None),
        P(),
        P("pipe", None),
        P("ep", None),
        P("ep", None, "pipe"),
        P("ep", "pipe", None),
    )
    return jax.shard_map(
        shards, mesh=mesh, in_specs=placed, out_specs=P("ep", "pipe"), check_vma=False
    )
```

time: 472 us -> 110 us (0.23)
  waiting for transfers between devices: 211 us -> 0 us
  blocking collectives: 185 us -> 0 us
  Pallas kernels: 0 us -> 104 us
  other arithmetic: 22.7 us -> 0 us
  matrix products: 14.6 us -> 0 us
  between operations: 13.6 us -> 0.01 us
  local copies, waits for them, and re-layouts: 15.8 us -> 3.08 us
  starting transfers between devices: 6.71 us -> 0 us
    all_to_all x1 -> x0, blocking collectives: 185 us -> none  [shards(): lax.all_to_all(outgoing, 'ep', split_axis=0, concat_axis=0, tiled=True)]
    psum x1 -> x0, waiting for transfers between devices: 128 us -> none  [shards(): lax.psum(partial_logits.astype(jnp.bfloat16), 'pipe').astype(jnp.float32)]
    pallas_call x0 -> x1, Pallas kernels: none -> 104 us  [shards(): pl.pallas_call(kernel, out_shape=jax.ShapeDtypeStruct((tok, width // PIPE...]
    reduce_scatter x1 -> x0, waiting for transfers between devices: 61.3 us -> none  [shards(): lax.psum_scatter(weighted.astype(jnp.bfloat16), 'pipe', scatter_dimension...]
    all_to_all x1 -> x0, waiting for transfers between devices: 22.6 us -> none  [shards(): lax.all_to_all(partial_value.reshape(sources, count, width), 'ep', split_...]
    dot_general x5 -> x0, matrix products: 14.6 us -> none  [the longest x1 7.33 us: shards(): jnp.dot(combining, flat_returned, preferred_element_type=jnp.float32, pre...]
    convert_element_type x4 -> x0, other arithmetic: 9.36 us -> none  [the longest x1 4.15 us: shards(): normed = (values * scale * norm_gain).astype(jnp.bfloat16)]
    another operation x2 -> x0, other arithmetic: 9.04 us -> none
  transfers between devices with their start and end apart: 3 -> 0, of which waited for: 3 -> 0; matrix products, arithmetic and copies ran while one was open for 3% -> 0% of each run, Pallas kernels for 0% -> 0%
where the time goes in v1:
time: 110 us; the launch traced here: 107 us
  Pallas kernels  104 us (95%)
  local copies, waits for them, and re-layouts  3.08 us (3%)
    pallas_call x1, Pallas kernels, shards(): pl.pallas_call(kernel, out_shape=jax.ShapeDtypeStruct((tok, width // PIPE...  104 us

profile of v1, /device:TPU:1, one launch (start us, length us, event | category | flops | bytes accessed | tf_op | source)
XLA Modules:
  0.0 107.5 jit_solution(14785615337477116794)
XLA Ops:
  0.0 1.4 %copy.7.routes_ref = s32[128,8]{1,0:T(8,128)} copy(s32[128,8]{0,1:T(8,128)} %param.9) | data formatting | bytes 8192 | tf_op args[3]
  1.4 104.4 %shard_map.64 = bf16[128,448]{1,0:T(8,128)(2,1)} custom-call(bf16[128,7168]{1,0:T(8,128)(2,1)} %tokens_hbm.1, f32[1,7168]{1,0:T(1,128)} %bitcast.1, bf16[448,256]{1,0:T(8,128)(2,1)} %router_hbm.1, s32[128,8]{1,0:T(8,128)} %copy.7.routes_ref, bf16[1,7168,128]{2,1,0:T(8,128)(2,1)} %gate_up_hbm.1, bf16[1,64,7168]{2,1,0:T(8,128)(2,1)} %down_hbm.1), custom_call_target="tpu_custom_call" | custom-call | flops 2000000000 | bytes 8000000 | tf_op jit(solution)/shard_map/pallas_call | solution.py:404
  105.8 1.7 %copy.8 = bf16[128,448]{0,1:T(8,128)(2,1)} copy(bf16[128,448]{1,0:T(8,128)(2,1)} %shard_map.64) | data formatting | bytes 229376 | tf_op jit(solution)/shard_map/pallas_call | solution.py:404

commit v2 on v1

v2 whole, which is shorter than its diff:
```python
import functools

import jax
import jax.numpy as jnp
from jax import lax
from jax.experimental import pallas as pl
from jax.experimental.pallas import tpu as pltpu
from jax.sharding import PartitionSpec as P

CORES = 2
NX = 4
NY = 2
CHIPS = NX * NY
PIPE = CHIPS * CORES
NZ = 16
HALVES = 2
CAP = 8
LANES = 128
MESH = pl.DeviceIdType.MESH


def remote(src, dst, send, recv, pipe, ep):
    return pltpu.make_async_remote_copy(
        src_ref=src,
        dst_ref=dst,
        send_sem=send,
        recv_sem=recv,
        device_id=(pipe, ep),
        device_id_type=MESH,
    )


def one_hot(names, first, count, width):
    row = lax.broadcasted_iota(jnp.int32, (width, names.shape[1]), 0)
    expert = first + row // count
    named = names[0:1, :] == expert
    for k in range(1, names.shape[0]):
        named = named | (names[k : k + 1, :] == expert)
    return jnp.where(named, 1.0, 0.0), row


def slot_matrix(names, first, width):
    named, row = one_hot(names, first, CAP, width)
    tok = names.shape[1]
    earlier = lax.broadcasted_iota(jnp.int32, (tok, tok), 0) < lax.broadcasted_iota(
        jnp.int32, (tok, tok), 1
    )
    rank = jnp.dot(
        named.astype(jnp.bfloat16),
        jnp.where(earlier, 1.0, 0.0).astype(jnp.bfloat16),
        preferred_element_type=jnp.float32,
    )
    return jnp.where(rank == (row % CAP).astype(jnp.float32), named, 0.0)


def kernel(
    tokens_hbm, gain_ref, router_hbm, routes_ref, gate_up_hbm, down_hbm, out_ref,
    tokens, router, gate_up, down,
    outbox, inbox, rows, hidden, back_out, back_in,
    score_out, score_in, weight_out, weight_in,
    load_sem, near_sem, out_sem, gather_send, gather_recv, pair_sem,
    down_sem, hidden_send, hidden_recv, back_sem, back_near,
    score_sem, weight_sem,
):
    pipe, ep = lax.axis_index("pipe"), lax.axis_index("ep")
    core, chip = lax.rem(pipe, CORES), lax.div(pipe, CORES)
    x, y = lax.rem(chip, NX), lax.div(chip, NX)
    z, side = lax.rem(ep, NZ), lax.div(ep, NZ)
    far_side = lax.rem(side + core, HALVES)
    partner = pipe + 1 - 2 * core
    tok, width = tokens.shape
    columns = width // CHIPS
    tiles = columns // LANES
    half = NZ * CAP
    own = columns // CORES
    units = down.shape[2]
    total_slots = HALVES * half

    def column_block(which):
        return pl.ds(pl.multiple_of(which * columns, LANES), columns)

    own_lanes = pl.ds(pl.multiple_of(core * 2 * units, LANES), 2 * units)
    loads = []
    for number, (src, dst) in enumerate(
        ((tokens_hbm, tokens), (router_hbm, router.at[pl.ds(core * own, own), :]),
         (gate_up_hbm.at[0], gate_up.at[:, own_lanes]),
         (down_hbm.at[0, :, column_block(chip)], down.at[chip, core]))
    ):
        if number == 1:
            router[...] = jnp.zeros_like(router)
        loads.append(pltpu.make_async_copy(src, dst, load_sem.at[number]))
        loads[-1].start()

    barrier = pltpu.get_barrier_semaphore()

    def greet_pipe(i, _):
        pl.semaphore_signal(
            barrier, inc=1, device_id=(lax.rem(pipe + i, PIPE), ep), device_id_type=MESH
        )
        return 0

    lax.fori_loop(1, PIPE, greet_pipe, 0)

    def greet_ep(i, _):
        other = lax.rem(z + i, NZ)
        for k in range(CORES):
            pl.semaphore_signal(
                barrier, inc=1,
                device_id=(CORES * chip + k, lax.rem(side + k, HALVES) * NZ + other),
                device_id_type=MESH,
            )
        return 0

    lax.fori_loop(1, NZ, greet_ep, 0)
    pl.semaphore_signal(
        barrier, inc=1,
        device_id=(CORES * chip + 1, (1 - side) * NZ + z), device_id_type=MESH,
    )

    @pl.when(core == 1)
    def _():
        pl.semaphore_signal(barrier, inc=1, device_id=(partner, ep), device_id_type=MESH)

    names = routes_ref[...]
    placing = slot_matrix(names, lax.rem(core + side, HALVES) * NZ, half).astype(jnp.bfloat16)

    loads[0].wait()
    squares = jnp.zeros((tok, LANES), jnp.float32)
    for at in range(width // LANES):
        values = tokens[:, at * LANES : (at + 1) * LANES].astype(jnp.float32)
        squares += values * values
    scale = lax.rsqrt(jnp.sum(squares, axis=1, keepdims=True) / width + 1e-06)
    block = column_block(chip)
    normed = (tokens[:, block].astype(jnp.float32) * scale * gain_ref[:, block]).astype(
        jnp.bfloat16
    )
    placed = jnp.dot(placing, normed, preferred_element_type=jnp.float32)
    pieces = [
        placed[:, at * LANES : (at + 1) * LANES].reshape(NZ, CAP, LANES)
        for at in range(tiles)
    ]
    pieces.append(jnp.zeros((NZ, CAP, LANES), jnp.float32))
    outbox[...] = jnp.concatenate(pieces, axis=1).astype(jnp.bfloat16)

    pl.semaphore_wait(barrier, PIPE - 1 + 2 * NZ - 1 + core)

    def dispatch(i, _):
        other = lax.rem(z + i, NZ)
        remote(
            outbox.at[other], inbox.at[z], out_sem.at[0], out_sem.at[1],
            pipe, far_side * NZ + other,
        ).start()
        return 0

    lax.fori_loop(1, NZ, dispatch, 0)
    near = remote(
        outbox.at[z], inbox.at[z], near_sem.at[0], near_sem.at[1], pipe, far_side * NZ + z
    )

    @pl.when(core == 1)
    def _():
        near.start()

    @pl.when(core == 0)
    def _():
        pltpu.make_async_copy(outbox.at[z], inbox.at[z], near_sem.at[1]).start()

    def chip_at(ry, rx):
        return lax.rem(y + ry, NY) * NX + lax.rem(x + rx, NX)

    relative = [(ry, rx) for rx in (2, 1, 3, 0) for ry in (1, 0) if (ry, rx) != (0, 0)]
    mirror = {(ry, rx): ry * NX + (NX - rx) % NX for ry, rx in relative}

    def down_to(ry, rx):
        return remote(
            down_hbm.at[0, :, column_block(chip_at(ry, rx))], down.at[chip, core],
            down_sem.at[ry * NX + rx], down_sem.at[CHIPS + mirror[ry, rx]],
            CORES * chip_at(ry, rx) + core, ep,
        )

    for ry, rx in relative:
        down_to(ry, rx).start()
    gate_up_pair = remote(
        gate_up_hbm.at[0], gate_up.at[:, own_lanes], pair_sem.at[0], pair_sem.at[1], partner, ep
    )
    gate_up_pair.start()

    loads[1].wait()
    scores = jnp.dot(normed, router[...], preferred_element_type=jnp.float32)
    score_out[...] = scores.reshape(score_out.shape)
    score_in[pipe] = score_out[pipe]

    def send_scores(i, _):
        other = lax.rem(pipe + i, PIPE)
        remote(
            score_out.at[other], score_in.at[pipe], score_sem.at[0], score_sem.at[1], other, ep
        ).start()
        return 0

    lax.fori_loop(1, PIPE, send_scores, 0)

    most = pl.ds(0, NZ - 1)
    pltpu.make_async_copy(inbox.at[most], inbox.at[most], out_sem.at[1]).wait()
    pltpu.make_async_copy(inbox.at[0], inbox.at[0], near_sem.at[1]).wait()
    arrived = inbox[...].astype(jnp.float32)
    for at in range(tiles):
        rows[chip, :, at * LANES : (at + 1) * LANES] = (
            arrived[:, at * CAP : (at + 1) * CAP, :].reshape(half, LANES).astype(jnp.bfloat16)
        )

    def gather_to(ry, rx):
        return remote(
            rows.at[chip], rows.at[chip],
            gather_send.at[ry * NX + rx], gather_recv.at[mirror[ry, rx]],
            CORES * chip_at(ry, rx) + core, ep,
        )

    for ry, rx in relative:
        gather_to(ry, rx).start()

    loads[3].wait()
    for ry, rx in relative:
        down_to(ry, rx).wait_recv()
    down_pair = remote(
        down.at[:, core], down.at[:, core], pair_sem.at[2], pair_sem.at[3], partner, ep
    )
    down_pair.start()

    most_pipe = pl.ds(0, PIPE - 1)
    pltpu.make_async_copy(score_in.at[most_pipe], score_in.at[most_pipe], score_sem.at[1]).wait()
    affinity = jax.nn.sigmoid(jnp.sum(score_in[...], axis=0))
    group, experts = affinity.shape
    pick_token = lax.broadcasted_iota(jnp.int32, (group, tok), 1)
    pick_row = lax.broadcasted_iota(jnp.int32, (group, tok), 0)
    pick = jnp.where(pick_token == pick_row + pipe * group, 1.0, 0.0).astype(jnp.bfloat16)
    chosen_all, _ = one_hot(names, 0, 1, experts)
    chosen = lax.dot_general(
        pick, chosen_all.astype(jnp.bfloat16), (((1,), (1,)), ((), ())),
        preferred_element_type=jnp.float32,
    )
    fraction = 2.5 * affinity / jnp.sum(chosen * affinity, axis=1, keepdims=True)
    spread_row = lax.broadcasted_iota(jnp.int32, (experts, total_slots), 0)
    spread_lane = lax.broadcasted_iota(jnp.int32, (experts, total_slots), 1)
    slot_expert = lax.rem(spread_lane // CAP + side * NZ, HALVES * NZ)
    weight_out[...] = jnp.dot(
        fraction, jnp.where(spread_row == slot_expert, 1.0, 0.0),
        preferred_element_type=jnp.float32, precision=lax.Precision.HIGHEST,
    )
    weight_in[pipe] = weight_out[...]

    def send_weights(i, _):
        other = lax.rem(pipe + i, PIPE)
        remote(weight_out, weight_in.at[pipe], weight_sem.at[0], weight_sem.at[1], other, ep).start()
        return 0

    lax.fori_loop(1, PIPE, send_weights, 0)

    loads[2].wait()
    gate_up_pair.wait_recv()

    def project(which):
        return jnp.dot(
            rows[which],
            gate_up[pl.ds(pl.multiple_of(which * columns, LANES), columns), :],
            preferred_element_type=jnp.float32,
        )

    order = [(1, 0), (0, 1), (0, 3), (1, 1), (1, 3), (0, 2), (1, 2)]
    both = project(chip)
    for ry, rx in order:
        gather_to(ry, (NX - rx) % NX).wait_recv()
        both += project(chip_at(ry, rx))
    parts = []
    for k in range(CORES):
        gate = both[:, 2 * k * units : (2 * k + 1) * units]
        upper = both[:, (2 * k + 1) * units : (2 * k + 2) * units]
        parts.append(gate / (1.0 + jnp.exp(-gate)) * upper)
    hidden[chip] = jnp.concatenate(parts, axis=1).astype(jnp.bfloat16)

    def hidden_to(ry, rx):
        return remote(
            hidden.at[chip], hidden.at[chip],
            hidden_send.at[ry * NX + rx], hidden_recv.at[mirror[ry, rx]],
            CORES * chip_at(ry, rx) + core, ep,
        )

    for ry, rx in relative:
        hidden_to(ry, rx).start()

    down_pair.wait_recv()

    def lower(which):
        return jnp.dot(
            hidden[which], down[which].reshape(CORES * units, columns),
            preferred_element_type=jnp.float32,
        )

    result = lower(chip)
    for ry, rx in order:
        hidden_to(ry, (NX - rx) % NX).wait_recv()
        result += lower(chip_at(ry, rx))

    for j in range(CORES):
        pieces = []
        for at in range(4):
            low = j * own + at * LANES
            high = min(low + LANES, (j + 1) * own)
            piece = result[:, low:high]
            if high - low < LANES:
                piece = jnp.concatenate(
                    [piece, jnp.zeros((half, LANES - (high - low)), jnp.float32)], axis=1
                )
            pieces.append(piece.reshape(NZ, CAP, LANES))
        back_out[j] = jnp.concatenate(pieces, axis=1).astype(jnp.bfloat16)

    def go_back(i, _):
        other = lax.rem(z + i, NZ)
        for j in range(CORES):
            remote(
                back_out.at[j, other], back_in.at[core, z], back_sem.at[0], back_sem.at[1],
                CORES * chip + j, far_side * NZ + other,
            ).start()
        return 0

    lax.fori_loop(1, NZ, go_back, 0)
    back_one = remote(
        back_out.at[1, z], back_in.at[core, z], back_near.at[1], back_near.at[2 + core],
        CORES * chip + 1, far_side * NZ + z,
    )
    back_zero = remote(
        back_out.at[0, z], back_in.at[core, z], back_near.at[0], back_near.at[2 + core],
        CORES * chip, far_side * NZ + z,
    )
    back_one.start()

    @pl.when(core == 1)
    def _():
        back_zero.start()

    @pl.when(core == 0)
    def _():
        pltpu.make_async_copy(
            back_out.at[0, z], back_in.at[core, z], back_near.at[2 + core]
        ).start()

    slots_all = slot_matrix(names, 0, total_slots)
    slots_now = jnp.where(
        side == 0, slots_all, jnp.concatenate([slots_all[half:], slots_all[:half]], axis=0)
    )
    pltpu.make_async_copy(
        weight_in.at[most_pipe], weight_in.at[most_pipe], weight_sem.at[1]
    ).wait()
    combining = jnp.transpose(slots_now) * weight_in[...].reshape(tok, total_slots)
    chip_tokens = tokens[:, block].astype(jnp.float32)
    padding = jnp.zeros((tok, 4 * LANES - own), jnp.float32)
    residual = jnp.where(
        core == 0, chip_tokens[:, : 4 * LANES],
        jnp.concatenate([chip_tokens[:, own:], padding], axis=1),
    )

    pltpu.make_async_copy(outbox.at[most], outbox.at[most], out_sem.at[0]).wait()

    @pl.when(core == 1)
    def _():
        near.wait_send()

    pltpu.make_async_copy(
        score_out.at[most_pipe], score_out.at[most_pipe], score_sem.at[0]
    ).wait()
    pltpu.make_async_copy(
        weight_in.at[most_pipe], weight_in.at[most_pipe], weight_sem.at[0]
    ).wait()
    for ry, rx in relative:
        down_to(ry, rx).wait_send()
        gather_to(ry, rx).wait_send()
        hidden_to(ry, rx).wait_send()
    gate_up_pair.wait_send()
    down_pair.wait_send()

    pltpu.make_async_copy(
        back_in.at[:, most], back_in.at[:, most], back_sem.at[1]
    ).wait()
    for k in range(HALVES):
        pltpu.make_async_copy(back_in.at[k, 0], back_in.at[k, 0], back_near.at[2 + k]).wait()
    returned = back_in[...].astype(jnp.float32)
    returned = jnp.concatenate(
        [
            returned[:, :, at * CAP : (at + 1) * CAP, :].reshape(total_slots, LANES)
            for at in range(4)
        ],
        axis=1,
    )
    mixed = residual + jnp.dot(
        combining, returned, preferred_element_type=jnp.float32, precision=lax.Precision.HIGHEST
    )
    out_ref[...] = jnp.transpose(mixed)[:own, :].astype(jnp.bfloat16)

    @pl.when(core == 1)
    def _():
        back_zero.wait_send()

    back_one.wait_send()
    pltpu.make_async_copy(back_out.at[:, most], back_out.at[:, most], back_sem.at[0]).wait()


def shards(tokens, norm_gain, router, routes, w_gate_up, w_down):
    tok, width = tokens.shape
    columns = width // CHIPS
    half = NZ * CAP
    units = w_down.shape[1]
    experts = router.shape[1]
    group = tok // PIPE
    bf16, f32 = jnp.bfloat16, jnp.float32
    dma = pltpu.SemaphoreType.DMA
    anywhere = pl.BlockSpec(memory_space=pl.ANY)
    vmem = pl.BlockSpec(memory_space=pltpu.VMEM)
    mixed = pl.pallas_call(
        kernel,
        out_shape=jax.ShapeDtypeStruct((width // PIPE, tok), bf16),
        in_specs=[anywhere, vmem, anywhere, vmem, anywhere, anywhere],
        out_specs=vmem,
        scratch_shapes=[
            pltpu.VMEM((tok, width), bf16),
            pltpu.VMEM((columns, experts), bf16),
            pltpu.VMEM((width, CORES * 2 * units), bf16),
            pltpu.VMEM((CHIPS, CORES, units, columns), bf16),
            pltpu.VMEM((NZ, 64, LANES), bf16),
            pltpu.VMEM((NZ, 64, LANES), bf16),
            pltpu.VMEM((CHIPS, half, columns), bf16),
            pltpu.VMEM((CHIPS, half, CORES * units), bf16),
            pltpu.VMEM((CORES, NZ, 32, LANES), bf16),
            pltpu.VMEM((HALVES, NZ, 32, LANES), bf16),
            pltpu.VMEM((PIPE, group, experts), f32),
            pltpu.VMEM((PIPE, group, experts), f32),
            pltpu.VMEM((group, 2 * half), f32),
            pltpu.VMEM((PIPE, group, 2 * half), f32),
            dma((4,)), dma((2,)), dma((2,)),
            dma((CHIPS,)), dma((CHIPS,)), dma((4,)),
            dma((2 * CHIPS,)), dma((CHIPS,)), dma((CHIPS,)),
            dma((2,)), dma((4,)), dma((2,)), dma((2,)),
        ],
        compiler_params=pltpu.CompilerParams(
            collective_id=0, has_side_effects=True, vmem_limit_bytes=56 * 1024 * 1024
        ),
        cost_estimate=pl.CostEstimate(
            flops=2_000_000_000, bytes_accessed=8_000_000, transcendentals=100_000
        ),
    )(tokens, norm_gain.reshape(1, width), router, routes.T, w_gate_up, w_down)
    return mixed.T


def solution(mesh):
    placed = (
        P("ep", None),
        P(),
        P("pipe", None),
        P("ep", None),
        P("ep", None, "pipe"),
        P("ep", "pipe", None),
    )
    return jax.shard_map(
        shards, mesh=mesh, in_specs=placed, out_specs=P("ep", "pipe"), check_vma=False
    )
```

time: 110 us -> 86 us (0.78); the launches traced: 107 us -> 85.8 us
  Pallas kernels: 104 us -> 84.3 us
  local copies, waits for them, and re-layouts: 3.08 us -> 1.55 us
    pallas_call x1, Pallas kernels: 104 us -> 84.3 us  [shards(): pl.pallas_call(kernel, out_shape=jax.ShapeDtypeStruct((width // PIPE, tok...]
    pallas_call x1 -> x0, local copies, waits for them, and re-layouts: 1.67 us -> none  [shards(): pl.pallas_call(kernel, out_shape=jax.ShapeDtypeStruct((tok, width // PIPE...]
where the time goes in v2:
time: 86 us; the launch traced here: 85.8 us
  Pallas kernels  84.3 us (98%)
  local copies, waits for them, and re-layouts  1.55 us (2%)
    pallas_call x1, Pallas kernels, shards(): pl.pallas_call(kernel, out_shape=jax.ShapeDtypeStruct((width // PIPE, tok...  84.3 us

profile of v2, /device:TPU:1, one launch (start us, length us, event | category | flops | bytes accessed | tf_op | source)
XLA Modules:
  0.0 85.8 jit_solution(518202871194649344)
XLA Ops:
  0.0 84.3 %shard_map.64 = bf16[448,128]{1,0:T(8,128)(2,1)} custom-call(bf16[128,7168]{1,0:T(8,128)(2,1)} %tokens_hbm.1, f32[1,7168]{1,0:T(1,128)} %bitcast.4, bf16[448,256]{1,0:T(8,128)(2,1)} %router_hbm.1, s32[8,128]{1,0:T(8,128)} %bitcast.5, bf16[1,7168,128]{2,1,0:T(8,128)(2,1)} %gate_up_hbm.1, bf16[1,64,7168]{2,1,0:T(8,128)(2,1)} %down_hbm.1), custom_call_target="tpu_custom_call" | custom-call | flops 2000000000 | bytes 8000000 | tf_op jit(solution)/shard_map/pallas_call | solution.py:417
  84.3 1.6 %copy.8 = bf16[128,448]{0,1:T(8,128)(2,1)} copy(bf16[128,448]{0,1:T(8,128)(2,1)} %bitcast.3) | data formatting | bytes 229376

commit v3 on v2

--- a/solution.py
+++ b/solution.py
@@ -15,6 +15,8 @@
 NZ = 16
 HALVES = 2
 CAP = 8
+PARTS = ((0, 4), (4, 3))
+PIECE = 32
 LANES = 128
 MESH = pl.DeviceIdType.MESH
 
@@ -56,7 +58,7 @@
 def kernel(
     tokens_hbm, gain_ref, router_hbm, routes_ref, gate_up_hbm, down_hbm, out_ref,
     tokens, router, gate_up, down,
-    outbox, inbox, rows, hidden, back_out, back_in,
+    outbox, inbox, rows_a, rows_b, hidden, back_out, back_in,
     score_out, score_in, weight_out, weight_in,
     load_sem, near_sem, out_sem, gather_send, gather_recv, pair_sem,
     down_sem, hidden_send, hidden_recv, back_sem, back_near,
@@ -80,16 +82,17 @@
         return pl.ds(pl.multiple_of(which * columns, LANES), columns)
 
     own_lanes = pl.ds(pl.multiple_of(core * 2 * units, LANES), 2 * units)
-    loads = []
-    for number, (src, dst) in enumerate(
-        ((tokens_hbm, tokens), (router_hbm, router.at[pl.ds(core * own, own), :]),
-         (gate_up_hbm.at[0], gate_up.at[:, own_lanes]),
-         (down_hbm.at[0, :, column_block(chip)], down.at[chip, core]))
-    ):
-        if number == 1:
-            router[...] = jnp.zeros_like(router)
-        loads.append(pltpu.make_async_copy(src, dst, load_sem.at[number]))
-        loads[-1].start()
+    quarter = width // 4
+    token_loads = [
+        pltpu.make_async_copy(
+            tokens_hbm.at[:, pl.ds(n * quarter, quarter)],
+            tokens.at[:, pl.ds(n * quarter, quarter)],
+            load_sem.at[3 + n],
+        )
+        for n in range(4)
+    ]
+    for load in token_loads:
+        load.start()
 
     barrier = pltpu.get_barrier_semaphore()
 
@@ -124,46 +127,68 @@
     names = routes_ref[...]
     placing = slot_matrix(names, lax.rem(core + side, HALVES) * NZ, half).astype(jnp.bfloat16)
 
-    loads[0].wait()
     squares = jnp.zeros((tok, LANES), jnp.float32)
-    for at in range(width // LANES):
-        values = tokens[:, at * LANES : (at + 1) * LANES].astype(jnp.float32)
-        squares += values * values
+    for n in range(4):
+        token_loads[n].wait()
+        for at in range(n * quarter // LANES, (n + 1) * quarter // LANES):
+            values = tokens[:, at * LANES : (at + 1) * LANES].astype(jnp.float32)
+            squares += values * values
+    router[...] = jnp.zeros_like(router)
+    loads = [
+        pltpu.make_async_copy(src, dst, load_sem.at[number])
+        for number, (src, dst) in enumerate(
+            ((router_hbm, router.at[pl.ds(core * own, own), :]),
+             (gate_up_hbm.at[0], gate_up.at[:, own_lanes]),
+             (down_hbm.at[0, :, column_block(chip)], down.at[chip, core]))
+        )
+    ]
+    for load in loads:
+        load.start()
     scale = lax.rsqrt(jnp.sum(squares, axis=1, keepdims=True) / width + 1e-06)
     block = column_block(chip)
     normed = (tokens[:, block].astype(jnp.float32) * scale * gain_ref[:, block]).astype(
         jnp.bfloat16
     )
     placed = jnp.dot(placing, normed, preferred_element_type=jnp.float32)
-    pieces = [
-        placed[:, at * LANES : (at + 1) * LANES].reshape(NZ, CAP, LANES)
-        for at in range(tiles)
-    ]
-    pieces.append(jnp.zeros((NZ, CAP, LANES), jnp.float32))
-    outbox[...] = jnp.concatenate(pieces, axis=1).astype(jnp.bfloat16)
+    for part, (first, count) in enumerate(PARTS):
+        pieces = [
+            placed[:, at * LANES : (at + 1) * LANES].reshape(NZ, CAP, LANES)
+            for at in range(first, first + count)
+        ]
+        if count < 4:
+            pieces.append(jnp.zeros((NZ, PIECE - count * CAP, LANES), jnp.float32))
+        outbox[part] = jnp.concatenate(pieces, axis=1).astype(jnp.bfloat16)
 
     pl.semaphore_wait(barrier, PIPE - 1 + 2 * NZ - 1 + core)
 
-    def dispatch(i, _):
-        other = lax.rem(z + i, NZ)
-        remote(
-            outbox.at[other], inbox.at[z], out_sem.at[0], out_sem.at[1],
-            pipe, far_side * NZ + other,
-        ).start()
-        return 0
-
-    lax.fori_loop(1, NZ, dispatch, 0)
-    near = remote(
-        outbox.at[z], inbox.at[z], near_sem.at[0], near_sem.at[1], pipe, far_side * NZ + z
-    )
+    near = []
+    for part in range(2):
+        def dispatch(i, _):
+            other = lax.rem(z + i, NZ)
+            remote(
+                outbox.at[part, other], inbox.at[part, z],
+                out_sem.at[2 * part], out_sem.at[2 * part + 1],
+                pipe, far_side * NZ + other,
+            ).start()
+            return 0
+
+        lax.fori_loop(1, NZ, dispatch, 0)
+        near.append(remote(
+            outbox.at[part, z], inbox.at[part, z],
+            near_sem.at[2 * part], near_sem.at[2 * part + 1], pipe, far_side * NZ + z,
+        ))
 
     @pl.when(core == 1)
     def _():
-        near.start()
+        for copy in near:
+            copy.start()
 
     @pl.when(core == 0)
     def _():
-        pltpu.make_async_copy(outbox.at[z], inbox.at[z], near_sem.at[1]).start()
+        for part in range(2):
+            pltpu.make_async_copy(
+                outbox.at[part, z], inbox.at[part, z], near_sem.at[2 * part + 1]
+            ).start()
 
     def chip_at(ry, rx):
         return lax.rem(y + ry, NY) * NX + lax.rem(x + rx, NX)
@@ -185,7 +210,7 @@
     )
     gate_up_pair.start()
 
-    loads[1].wait()
+    loads[0].wait()
     scores = jnp.dot(normed, router[...], preferred_element_type=jnp.float32)
     score_out[...] = scores.reshape(score_out.shape)
     score_in[pipe] = score_out[pipe]
@@ -200,25 +225,64 @@
     lax.fori_loop(1, PIPE, send_scores, 0)
 
     most = pl.ds(0, NZ - 1)
-    pltpu.make_async_copy(inbox.at[most], inbox.at[most], out_sem.at[1]).wait()
-    pltpu.make_async_copy(inbox.at[0], inbox.at[0], near_sem.at[1]).wait()
-    arrived = inbox[...].astype(jnp.float32)
-    for at in range(tiles):
-        rows[chip, :, at * LANES : (at + 1) * LANES] = (
-            arrived[:, at * CAP : (at + 1) * CAP, :].reshape(half, LANES).astype(jnp.bfloat16)
-        )
-
-    def gather_to(ry, rx):
-        return remote(
-            rows.at[chip], rows.at[chip],
-            gather_send.at[ry * NX + rx], gather_recv.at[mirror[ry, rx]],
-            CORES * chip_at(ry, rx) + core, ep,
-        )
-
-    for ry, rx in relative:
-        gather_to(ry, rx).start()
-
-    loads[3].wait()
+    gathered = (rows_a, rows_b)
+    sent = []
+
+    def arrive(part):
+        first, count = PARTS[part]
+        pltpu.make_async_copy(
+            inbox.at[part, most], inbox.at[part, most], out_sem.at[2 * part + 1]
+        ).wait()
+        pltpu.make_async_copy(
+            inbox.at[part, 0], inbox.at[part, 0], near_sem.at[2 * part + 1]
+        ).wait()
+        arrived = inbox[part].astype(jnp.float32)
+        for at in range(count):
+            gathered[part][chip, :, at * LANES : (at + 1) * LANES] = (
+                arrived[:, at * CAP : (at + 1) * CAP, :].reshape(half, LANES).astype(jnp.bfloat16)
+            )
+
+    def block_ref(part, ry, rx, piece):
+        ref = gathered[part].at[chip_at(ry, rx)]
+        return ref if piece is None else ref.at[pl.ds(piece * (half // 2), half // 2), :]
+
+    def recv_sem(part, ry, rx, piece):
+        return gather_recv.at[(part * CHIPS + (ry % NY) * NX + rx % NX) * 2 + (piece or 0)]
+
+    def pass_on(part, block, target, piece=None):
+        (ry, rx), (ty, tx) = block, target
+        ref = block_ref(part, ry, rx, piece)
+        copy = remote(
+            ref, ref, gather_send.at[len(sent)], recv_sem(part, ry + ty, rx - tx + NX, piece),
+            CORES * chip_at(ty, tx) + core, ep,
+        )
+        copy.start()
+        sent.append(copy)
+
+    def take(part, ry, rx, piece=None):
+        ref = block_ref(part, ry, rx, piece)
+        pltpu.make_async_copy(ref, ref, recv_sem(part, ry, rx, piece)).wait()
+
+    up, plus, minus = (1, 0), (0, 1), (0, 3)
+
+    arrive(0)
+    for target in (plus, minus, up):
+        pass_on(0, (0, 0), target)
+
+    take(0, 1, 0)
+    pass_on(0, (1, 0), plus)
+    pass_on(0, (1, 0), minus)
+    for ry in range(NY):
+        take(0, ry, 3)
+        pass_on(0, (ry, 3), plus, 0)
+        take(0, ry, 1)
+        pass_on(0, (ry, 1), minus, 1)
+
+    arrive(1)
+    for target in (plus, minus, up):
+        pass_on(1, (0, 0), target)
+
+    loads[2].wait()
     for ry, rx in relative:
         down_to(ry, rx).wait_recv()
     down_pair = remote(
@@ -255,21 +319,41 @@
 
     lax.fori_loop(1, PIPE, send_weights, 0)
 
-    loads[2].wait()
+    loads[1].wait()
     gate_up_pair.wait_recv()
 
-    def project(which):
+    def project(part, ry, rx):
+        first, count = PARTS[part]
+        which = chip_at(ry, rx)
+        start = pl.multiple_of(which * columns + first * LANES, LANES)
         return jnp.dot(
-            rows[which],
-            gate_up[pl.ds(pl.multiple_of(which * columns, LANES), columns), :],
+            gathered[part][which], gate_up[pl.ds(start, count * LANES), :],
             preferred_element_type=jnp.float32,
         )
 
-    order = [(1, 0), (0, 1), (0, 3), (1, 1), (1, 3), (0, 2), (1, 2)]
-    both = project(chip)
-    for ry, rx in order:
-        gather_to(ry, (NX - rx) % NX).wait_recv()
-        both += project(chip_at(ry, rx))
+    both = project(0, 0, 0) + project(0, 1, 0)
+    take(1, 0, 3)
+    pass_on(1, (0, 3), plus, 0)
+    pass_on(1, (0, 3), up)
+    take(1, 0, 1)
+    pass_on(1, (0, 1), minus, 1)
+    pass_on(1, (0, 1), up)
+    for ry in range(NY):
+        both += project(0, ry, 3) + project(0, ry, 1)
+    for piece in range(2):
+        take(1, 0, 2, piece)
+        pass_on(1, (0, 2), up, piece)
+    both += project(1, 0, 0) + project(1, 0, 1) + project(1, 0, 2) + project(1, 0, 3)
+    for ry in range(NY):
+        for piece in range(2):
+            take(0, ry, 2, piece)
+        both += project(0, ry, 2)
+    for rx in (0, 3, 1):
+        take(1, 1, rx)
+        both += project(1, 1, rx)
+    for piece in range(2):
+        take(1, 1, 2, piece)
+    both += project(1, 1, 2)
     parts = []
     for k in range(CORES):
         gate = both[:, 2 * k * units : (2 * k + 1) * units]
@@ -295,6 +379,7 @@
             preferred_element_type=jnp.float32,
         )
 
+    order = [(1, 0), (0, 1), (0, 3), (1, 1), (1, 3), (0, 2), (1, 2)]
     result = lower(chip)
     for ry, rx in order:
         hidden_to(ry, (NX - rx) % NX).wait_recv()
@@ -358,11 +443,15 @@
         jnp.concatenate([chip_tokens[:, own:], padding], axis=1),
     )
 
-    pltpu.make_async_copy(outbox.at[most], outbox.at[most], out_sem.at[0]).wait()
+    for part in range(2):
+        pltpu.make_async_copy(
+            outbox.at[part, most], outbox.at[part, most], out_sem.at[2 * part]
+        ).wait()
 
     @pl.when(core == 1)
     def _():
-        near.wait_send()
+        for copy in near:
+            copy.wait_send()
 
     pltpu.make_async_copy(
         score_out.at[most_pipe], score_out.at[most_pipe], score_sem.at[0]
@@ -372,8 +461,9 @@
     ).wait()
     for ry, rx in relative:
         down_to(ry, rx).wait_send()
-        gather_to(ry, rx).wait_send()
         hidden_to(ry, rx).wait_send()
+    for copy in sent:
+        copy.wait_send()
     gate_up_pair.wait_send()
     down_pair.wait_send()
 
@@ -424,9 +514,10 @@
             pltpu.VMEM((columns, experts), bf16),
             pltpu.VMEM((width, CORES * 2 * units), bf16),
             pltpu.VMEM((CHIPS, CORES, units, columns), bf16),
-            pltpu.VMEM((NZ, 64, LANES), bf16),
-            pltpu.VMEM((NZ, 64, LANES), bf16),
-            pltpu.VMEM((CHIPS, half, columns), bf16),
+            pltpu.VMEM((2, NZ, PIECE, LANES), bf16),
+            pltpu.VMEM((2, NZ, PIECE, LANES), bf16),
+            pltpu.VMEM((CHIPS, half, PARTS[0][1] * LANES), bf16),
+            pltpu.VMEM((CHIPS, half, PARTS[1][1] * LANES), bf16),
             pltpu.VMEM((CHIPS, half, CORES * units), bf16),
             pltpu.VMEM((CORES, NZ, 32, LANES), bf16),
             pltpu.VMEM((HALVES, NZ, 32, LANES), bf16),
@@ -434,8 +525,8 @@
             pltpu.VMEM((PIPE, group, experts), f32),
             pltpu.VMEM((group, 2 * half), f32),
             pltpu.VMEM((PIPE, group, 2 * half), f32),
-            dma((4,)), dma((2,)), dma((2,)),
-            dma((CHIPS,)), dma((CHIPS,)), dma((4,)),
+            dma((7,)), dma((4,)), dma((4,)),
+            dma((32,)), dma((4 * CHIPS,)), dma((4,)),
             dma((2 * CHIPS,)), dma((CHIPS,)), dma((CHIPS,)),
             dma((2,)), dma((4,)), dma((2,)), dma((2,)),
         ],

time: 86 us -> 80.4 us (0.935)
  Pallas kernels: 84.3 us -> 77.8 us
    pallas_call x1, Pallas kernels: 84.3 us -> 77.8 us  [shards(): pl.pallas_call(kernel, out_shape=jax.ShapeDtypeStruct((width // PIPE, tok...]
where the time goes in v3:
time: 80.4 us; the launch traced here: 79.4 us
  Pallas kernels  77.8 us (97%)
  local copies, waits for them, and re-layouts  1.55 us (2%)
    pallas_call x1, Pallas kernels, shards(): pl.pallas_call(kernel, out_shape=jax.ShapeDtypeStruct((width // PIPE, tok...  77.8 us

profile of v3, /device:TPU:1, one launch (start us, length us, event | category | flops | bytes accessed | tf_op | source)
XLA Modules:
  0.0 79.4 jit_solution(6491184749084485588)
XLA Ops:
  0.0 77.8 %shard_map.64 = bf16[448,128]{1,0:T(8,128)(2,1)} custom-call(bf16[128,7168]{1,0:T(8,128)(2,1)} %tokens_hbm.1, f32[1,7168]{1,0:T(1,128)} %bitcast.4, bf16[448,256]{1,0:T(8,128)(2,1)} %router_hbm.1, s32[8,128]{1,0:T(8,128)} %bitcast.5, bf16[1,7168,128]{2,1,0:T(8,128)(2,1)} %gate_up_hbm.1, bf16[1,64,7168]{2,1,0:T(8,128)(2,1)} %down_hbm.1), custom_call_target="tpu_custom_call" | custom-call | flops 2000000000 | bytes 8000000 | tf_op jit(solution)/shard_map/pallas_call | solution.py:507
  77.8 1.6 %copy.8 = bf16[128,448]{0,1:T(8,128)(2,1)} copy(bf16[128,448]{0,1:T(8,128)(2,1)} %bitcast.3) | data formatting | bytes 229376

commit v4 on v3

--- a/solution.py
+++ b/solution.py
@@ -57,7 +57,7 @@
 
 def kernel(
     tokens_hbm, gain_ref, router_hbm, routes_ref, gate_up_hbm, down_hbm, out_ref,
-    tokens, router, gate_up, down,
+    tokens, router, gate_up, down_a, down_b,
     outbox, inbox, rows_a, rows_b, hidden, back_out, back_in,
     score_out, score_in, weight_out, weight_in,
     load_sem, near_sem, out_sem, gather_send, gather_recv, pair_sem,
@@ -75,11 +75,20 @@
     tiles = columns // LANES
     half = NZ * CAP
     own = columns // CORES
-    units = down.shape[2]
+    units = down_a.shape[2]
+    downs = (down_a, down_b)
     total_slots = HALVES * half
 
     def column_block(which):
         return pl.ds(pl.multiple_of(which * columns, LANES), columns)
+
+    def down_columns(part, which):
+        first, count = PARTS[part]
+        start = pl.multiple_of(which * columns + first * LANES, LANES)
+        return down_hbm.at[0, :, pl.ds(start, count * LANES)]
+
+    def far_first(i):
+        return lax.rem(z + NZ // 2 + lax.div(i, 2) * (1 - 2 * lax.rem(i, 2)), NZ)
 
     own_lanes = pl.ds(pl.multiple_of(core * 2 * units, LANES), 2 * units)
     quarter = width // 4
@@ -87,7 +96,7 @@
         pltpu.make_async_copy(
             tokens_hbm.at[:, pl.ds(n * quarter, quarter)],
             tokens.at[:, pl.ds(n * quarter, quarter)],
-            load_sem.at[3 + n],
+            load_sem.at[4 + n],
         )
         for n in range(4)
     ]
@@ -139,7 +148,8 @@
         for number, (src, dst) in enumerate(
             ((router_hbm, router.at[pl.ds(core * own, own), :]),
              (gate_up_hbm.at[0], gate_up.at[:, own_lanes]),
-             (down_hbm.at[0, :, column_block(chip)], down.at[chip, core]))
+             (down_columns(0, chip), down_a.at[chip, core]),
+             (down_columns(1, chip), down_b.at[chip, core]))
         )
     ]
     for load in loads:
@@ -161,10 +171,15 @@
 
     pl.semaphore_wait(barrier, PIPE - 1 + 2 * NZ - 1 + core)
 
-    near = []
-    for part in range(2):
+    def near_copy(part):
+        return remote(
+            outbox.at[part, z], inbox.at[part, z],
+            near_sem.at[2 * part], near_sem.at[2 * part + 1], pipe, far_side * NZ + z,
+        )
+
+    def send_rows(part):
         def dispatch(i, _):
-            other = lax.rem(z + i, NZ)
+            other = far_first(i)
             remote(
                 outbox.at[part, other], inbox.at[part, z],
                 out_sem.at[2 * part], out_sem.at[2 * part + 1],
@@ -173,38 +188,56 @@
             return 0
 
         lax.fori_loop(1, NZ, dispatch, 0)
-        near.append(remote(
-            outbox.at[part, z], inbox.at[part, z],
-            near_sem.at[2 * part], near_sem.at[2 * part + 1], pipe, far_side * NZ + z,
-        ))
-
-    @pl.when(core == 1)
-    def _():
-        for copy in near:
-            copy.start()
-
-    @pl.when(core == 0)
-    def _():
-        for part in range(2):
+
+        @pl.when(core == 1)
+        def _():
+            near_copy(part).start()
+
+        @pl.when(core == 0)
+        def _():
             pltpu.make_async_copy(
                 outbox.at[part, z], inbox.at[part, z], near_sem.at[2 * part + 1]
             ).start()
 
+    def rows_left(part):
+        pltpu.make_async_copy(
+            outbox.at[part, most], outbox.at[part, most], out_sem.at[2 * part]
+        ).wait()
+
+        @pl.when(core == 1)
+        def _():
+            near_copy(part).wait_send()
+
+    most = pl.ds(0, NZ - 1)
+    send_rows(0)
+
     def chip_at(ry, rx):
         return lax.rem(y + ry, NY) * NX + lax.rem(x + rx, NX)
 
     relative = [(ry, rx) for rx in (2, 1, 3, 0) for ry in (1, 0) if (ry, rx) != (0, 0)]
     mirror = {(ry, rx): ry * NX + (NX - rx) % NX for ry, rx in relative}
 
-    def down_to(ry, rx):
+    def down_to(part, ry, rx):
         return remote(
-            down_hbm.at[0, :, column_block(chip_at(ry, rx))], down.at[chip, core],
-            down_sem.at[ry * NX + rx], down_sem.at[CHIPS + mirror[ry, rx]],
+            down_columns(part, chip_at(ry, rx)), downs[part].at[chip, core],
+            down_sem.at[part, ry * NX + rx], down_sem.at[part, CHIPS + mirror[ry, rx]],
             CORES * chip_at(ry, rx) + core, ep,
         )
 
+    def down_pair(part):
+        return remote(
+            downs[part].at[:, core], downs[part].at[:, core],
+            pair_sem.at[2 + 2 * part], pair_sem.at[3 + 2 * part], partner, ep,
+        )
+
+    def share_down(part):
+        loads[2 + part].wait()
+        for ry, rx in relative:
+            down_to(part, ry, rx).wait_recv()
+        down_pair(part).start()
+
     for ry, rx in relative:
-        down_to(ry, rx).start()
+        down_to(0, ry, rx).start()
     gate_up_pair = remote(
         gate_up_hbm.at[0], gate_up.at[:, own_lanes], pair_sem.at[0], pair_sem.at[1], partner, ep
     )
@@ -224,7 +257,9 @@
 
     lax.fori_loop(1, PIPE, send_scores, 0)
 
-    most = pl.ds(0, NZ - 1)
+    rows_left(0)
+    send_rows(1)
+
     gathered = (rows_a, rows_b)
     sent = []
 
@@ -282,13 +317,7 @@
     for target in (plus, minus, up):
         pass_on(1, (0, 0), target)
 
-    loads[2].wait()
-    for ry, rx in relative:
-        down_to(ry, rx).wait_recv()
-    down_pair = remote(
-        down.at[:, core], down.at[:, core], pair_sem.at[2], pair_sem.at[3], partner, ep
-    )
-    down_pair.start()
+    share_down(0)
 
     most_pipe = pl.ds(0, PIPE - 1)
     pltpu.make_async_copy(score_in.at[most_pipe], score_in.at[most_pipe], score_sem.at[1]).wait()
@@ -343,6 +372,8 @@
     for piece in range(2):
         take(1, 0, 2, piece)
         pass_on(1, (0, 2), up, piece)
+    for ry, rx in relative:
+        down_to(1, ry, rx).start()
     both += project(1, 0, 0) + project(1, 0, 1) + project(1, 0, 2) + project(1, 0, 3)
     for ry in range(NY):
         for piece in range(2):
@@ -371,25 +402,20 @@
     for ry, rx in relative:
         hidden_to(ry, rx).start()
 
-    down_pair.wait_recv()
-
-    def lower(which):
+    down_pair(0).wait_recv()
+    order = [(1, 0), (0, 1), (0, 3), (1, 1), (1, 3), (0, 2), (1, 2)]
+
+    def lower(part, ry, rx):
+        which = chip_at(ry, rx)
         return jnp.dot(
-            hidden[which], down[which].reshape(CORES * units, columns),
+            hidden[which], downs[part][which].reshape(CORES * units, PARTS[part][1] * LANES),
             preferred_element_type=jnp.float32,
         )
 
-    order = [(1, 0), (0, 1), (0, 3), (1, 1), (1, 3), (0, 2), (1, 2)]
-    result = lower(chip)
-    for ry, rx in order:
-        hidden_to(ry, (NX - rx) % NX).wait_recv()
-        result += lower(chip_at(ry, rx))
-
-    for j in range(CORES):
+    def go_back(j, result):
         pieces = []
         for at in range(4):
-            low = j * own + at * LANES
-            high = min(low + LANES, (j + 1) * own)
+            low, high = at * LANES, min((at + 1) * LANES, own)
             piece = result[:, low:high]
             if high - low < LANES:
                 piece = jnp.concatenate(
@@ -398,25 +424,25 @@
             pieces.append(piece.reshape(NZ, CAP, LANES))
         back_out[j] = jnp.concatenate(pieces, axis=1).astype(jnp.bfloat16)
 
-    def go_back(i, _):
-        other = lax.rem(z + i, NZ)
-        for j in range(CORES):
+        def go(i, _):
+            other = far_first(i)
             remote(
                 back_out.at[j, other], back_in.at[core, z], back_sem.at[0], back_sem.at[1],
                 CORES * chip + j, far_side * NZ + other,
             ).start()
-        return 0
-
-    lax.fori_loop(1, NZ, go_back, 0)
-    back_one = remote(
-        back_out.at[1, z], back_in.at[core, z], back_near.at[1], back_near.at[2 + core],
-        CORES * chip + 1, far_side * NZ + z,
-    )
+            return 0
+
+        lax.fori_loop(1, NZ, go, 0)
+
+    low_part = lower(0, 0, 0)
+    for ry, rx in order:
+        hidden_to(ry, (NX - rx) % NX).wait_recv()
+        low_part += lower(0, ry, rx)
+    go_back(0, low_part)
     back_zero = remote(
         back_out.at[0, z], back_in.at[core, z], back_near.at[0], back_near.at[2 + core],
         CORES * chip, far_side * NZ + z,
     )
-    back_one.start()
 
     @pl.when(core == 1)
     def _():
@@ -427,6 +453,18 @@
         pltpu.make_async_copy(
             back_out.at[0, z], back_in.at[core, z], back_near.at[2 + core]
         ).start()
+
+    share_down(1)
+    down_pair(1).wait_recv()
+    high_part = lower(1, 0, 0)
+    for ry, rx in order:
+        high_part += lower(1, ry, rx)
+    go_back(1, jnp.concatenate([low_part[:, own:], high_part], axis=1))
+    back_one = remote(
+        back_out.at[1, z], back_in.at[core, z], back_near.at[1], back_near.at[2 + core],
+        CORES * chip + 1, far_side * NZ + z,
+    )
+    back_one.start()
 
     slots_all = slot_matrix(names, 0, total_slots)
     slots_now = jnp.where(
@@ -443,16 +481,7 @@
         jnp.concatenate([chip_tokens[:, own:], padding], axis=1),
     )
 
-    for part in range(2):
-        pltpu.make_async_copy(
-            outbox.at[part, most], outbox.at[part, most], out_sem.at[2 * part]
-        ).wait()
-
-    @pl.when(core == 1)
-    def _():
-        for copy in near:
-            copy.wait_send()
-
+    rows_left(1)
     pltpu.make_async_copy(
         score_out.at[most_pipe], score_out.at[most_pipe], score_sem.at[0]
     ).wait()
@@ -460,12 +489,14 @@
         weight_in.at[most_pipe], weight_in.at[most_pipe], weight_sem.at[0]
     ).wait()
     for ry, rx in relative:
-        down_to(ry, rx).wait_send()
+        down_to(0, ry, rx).wait_send()
+        down_to(1, ry, rx).wait_send()
         hidden_to(ry, rx).wait_send()
     for copy in sent:
         copy.wait_send()
     gate_up_pair.wait_send()
-    down_pair.wait_send()
+    down_pair(0).wait_send()
+    down_pair(1).wait_send()
 
     pltpu.make_async_copy(
         back_in.at[:, most], back_in.at[:, most], back_sem.at[1]
@@ -513,7 +544,8 @@
             pltpu.VMEM((tok, width), bf16),
             pltpu.VMEM((columns, experts), bf16),
             pltpu.VMEM((width, CORES * 2 * units), bf16),
-            pltpu.VMEM((CHIPS, CORES, units, columns), bf16),
+            pltpu.VMEM((CHIPS, CORES, units, PARTS[0][1] * LANES), bf16),
+            pltpu.VMEM((CHIPS, CORES, units, PARTS[1][1] * LANES), bf16),
             pltpu.VMEM((2, NZ, PIECE, LANES), bf16),
             pltpu.VMEM((2, NZ, PIECE, LANES), bf16),
             pltpu.VMEM((CHIPS, half, PARTS[0][1] * LANES), bf16),
@@ -525,9 +557,9 @@
             pltpu.VMEM((PIPE, group, experts), f32),
             pltpu.VMEM((group, 2 * half), f32),
             pltpu.VMEM((PIPE, group, 2 * half), f32),
-            dma((7,)), dma((4,)), dma((4,)),
-            dma((32,)), dma((4 * CHIPS,)), dma((4,)),
-            dma((2 * CHIPS,)), dma((CHIPS,)), dma((CHIPS,)),
+            dma((8,)), dma((4,)), dma((4,)),
+            dma((32,)), dma((4 * CHIPS,)), dma((6,)),
+            dma((2, 2 * CHIPS)), dma((CHIPS,)), dma((CHIPS,)),
             dma((2,)), dma((4,)), dma((2,)), dma((2,)),
         ],
         compiler_params=pltpu.CompilerParams(

time: 80.4 us -> 80.1 us (level); the launches traced: 79.4 us -> 79.9 us
  no operation moved by 1% of the time
where the time goes in v4:
time: 80.1 us; the launch traced here: 79.9 us
  Pallas kernels  78.3 us (98%)
  local copies, waits for them, and re-layouts  1.55 us (2%)
    pallas_call x1, Pallas kernels, shards(): pl.pallas_call(kernel, out_shape=jax.ShapeDtypeStruct((width // PIPE, tok...  78.3 us

profile of v4, /device:TPU:1, one launch (start us, length us, event | category | flops | bytes accessed | tf_op | source)
XLA Modules:
  0.0 79.9 jit_solution(17360806121220474638)
XLA Ops:
  0.0 78.3 %shard_map.64 = bf16[448,128]{1,0:T(8,128)(2,1)} custom-call(bf16[128,7168]{1,0:T(8,128)(2,1)} %tokens_hbm.1, f32[1,7168]{1,0:T(1,128)} %bitcast.4, bf16[448,256]{1,0:T(8,128)(2,1)} %router_hbm.1, s32[8,128]{1,0:T(8,128)} %bitcast.5, bf16[1,7168,128]{2,1,0:T(8,128)(2,1)} %gate_up_hbm.1, bf16[1,64,7168]{2,1,0:T(8,128)(2,1)} %down_hbm.1), custom_call_target="tpu_custom_call" | custom-call | flops 2000000000 | bytes 8000000 | tf_op jit(solution)/shard_map/pallas_call | solution.py:538
  78.4 1.6 %copy.8 = bf16[128,448]{0,1:T(8,128)(2,1)} copy(bf16[128,448]{0,1:T(8,128)(2,1)} %bitcast.3) | data formatting | bytes 229376

commit v5 on v4

--- a/solution.py
+++ b/solution.py
@@ -15,8 +15,20 @@
 NZ = 16
 HALVES = 2
 CAP = 8
-PARTS = ((0, 4), (4, 3))
-PIECE = 32
+PARTS = ((0, 2), (2, 2), (4, 2), (6, 1))
+DOWN_PARTS = ((0, 4), (4, 3))
+PIECE = 16
+Y_FIRST = (0, 2)
+ARRIVALS = (
+    (0, 0, 0, None), (1, 0, 0, None), (0, 1, 0, None), (0, 0, 3, None), (0, 0, 1, None),
+    (2, 0, 0, None), (1, 0, 3, None), (1, 0, 1, None), (1, 1, 0, None), (0, 1, 3, None),
+    (0, 1, 1, None), (3, 0, 0, None), (0, 0, 2, 0), (0, 0, 2, 1), (2, 1, 0, None),
+    (2, 0, 3, None), (2, 0, 1, None), (1, 1, 3, None), (1, 0, 2, 0), (1, 0, 2, 1),
+    (0, 1, 2, 0), (0, 1, 2, 1), (1, 1, 1, None), (3, 0, 3, None), (3, 0, 1, None),
+    (3, 1, 0, None), (2, 1, 3, None), (2, 1, 1, None), (1, 1, 2, 0), (1, 1, 2, 1),
+    (2, 0, 2, 0), (2, 0, 2, 1), (3, 0, 2, 0), (3, 0, 2, 1), (3, 1, 3, None),
+    (3, 1, 1, None), (2, 1, 2, 0), (2, 1, 2, 1), (3, 1, 2, 0), (3, 1, 2, 1),
+)
 LANES = 128
 MESH = pl.DeviceIdType.MESH
 
@@ -58,7 +70,7 @@
 def kernel(
     tokens_hbm, gain_ref, router_hbm, routes_ref, gate_up_hbm, down_hbm, out_ref,
     tokens, router, gate_up, down_a, down_b,
-    outbox, inbox, rows_a, rows_b, hidden, back_out, back_in,
+    outbox, inbox, rows_a, rows_b, rows_c, rows_d, hidden, back_out, back_in,
     score_out, score_in, weight_out, weight_in,
     load_sem, near_sem, out_sem, gather_send, gather_recv, pair_sem,
     down_sem, hidden_send, hidden_recv, back_sem, back_near,
@@ -83,7 +95,7 @@
         return pl.ds(pl.multiple_of(which * columns, LANES), columns)
 
     def down_columns(part, which):
-        first, count = PARTS[part]
+        first, count = DOWN_PARTS[part]
         start = pl.multiple_of(which * columns + first * LANES, LANES)
         return down_hbm.at[0, :, pl.ds(start, count * LANES)]
 
@@ -165,7 +177,7 @@
             placed[:, at * LANES : (at + 1) * LANES].reshape(NZ, CAP, LANES)
             for at in range(first, first + count)
         ]
-        if count < 4:
+        if count * CAP < PIECE:
             pieces.append(jnp.zeros((NZ, PIECE - count * CAP, LANES), jnp.float32))
         outbox[part] = jnp.concatenate(pieces, axis=1).astype(jnp.bfloat16)
 
@@ -257,10 +269,11 @@
 
     lax.fori_loop(1, PIPE, send_scores, 0)
 
-    rows_left(0)
-    send_rows(1)
-
-    gathered = (rows_a, rows_b)
+    for part in range(1, len(PARTS) - 1):
+        rows_left(part - 1)
+        send_rows(part)
+
+    gathered = (rows_a, rows_b, rows_c, rows_d)
     sent = []
 
     def arrive(part):
@@ -300,24 +313,64 @@
 
     up, plus, minus = (1, 0), (0, 1), (0, 3)
 
-    arrive(0)
-    for target in (plus, minus, up):
-        pass_on(0, (0, 0), target)
-
-    take(0, 1, 0)
-    pass_on(0, (1, 0), plus)
-    pass_on(0, (1, 0), minus)
-    for ry in range(NY):
-        take(0, ry, 3)
-        pass_on(0, (ry, 3), plus, 0)
-        take(0, ry, 1)
-        pass_on(0, (ry, 1), minus, 1)
-
-    arrive(1)
-    for target in (plus, minus, up):
-        pass_on(1, (0, 0), target)
-
-    share_down(0)
+    def project(part, ry, rx):
+        first, count = PARTS[part]
+        which = chip_at(ry, rx)
+        start = pl.multiple_of(which * columns + first * LANES, LANES)
+        return jnp.dot(
+            gathered[part][which], gate_up[pl.ds(start, count * LANES), :],
+            preferred_element_type=jnp.float32,
+        )
+
+    both = jnp.zeros((half, CORES * 2 * units), jnp.float32)
+    for step, (part, ry, rx, piece) in enumerate(ARRIVALS):
+        here = (ry, rx)
+        if here == (0, 0):
+            arrive(part)
+            for target in (up, plus, minus) if part in Y_FIRST else (plus, minus, up):
+                pass_on(part, here, target)
+        else:
+            take(part, ry, rx, piece)
+            if part in Y_FIRST:
+                if here == up:
+                    pass_on(part, here, plus)
+                    pass_on(part, here, minus)
+            elif ry == 0 and rx == 2:
+                pass_on(part, here, up, piece)
+            if part in Y_FIRST or ry == 0:
+                if rx == 3:
+                    pass_on(part, here, plus, 0)
+                elif rx == 1:
+                    pass_on(part, here, minus, 1)
+            if part not in Y_FIRST and ry == 0 and rx != 2:
+                pass_on(part, here, up)
+        if step == 0:
+            rows_left(len(PARTS) - 2)
+            send_rows(len(PARTS) - 1)
+            loads[1].wait()
+            gate_up_pair.wait_recv()
+        if (part, ry, rx) == (len(PARTS) - 1, 0, 0):
+            share_down(0)
+        if piece != 0:
+            both += project(part, ry, rx)
+    parts = []
+    for k in range(CORES):
+        gate = both[:, 2 * k * units : (2 * k + 1) * units]
+        upper = both[:, (2 * k + 1) * units : (2 * k + 2) * units]
+        parts.append(gate / (1.0 + jnp.exp(-gate)) * upper)
+    hidden[chip] = jnp.concatenate(parts, axis=1).astype(jnp.bfloat16)
+
+    def hidden_to(ry, rx):
+        return remote(
+            hidden.at[chip], hidden.at[chip],
+            hidden_send.at[ry * NX + rx], hidden_recv.at[mirror[ry, rx]],
+            CORES * chip_at(ry, rx) + core, ep,
+        )
+
+    for ry, rx in relative:
+        hidden_to(ry, rx).start()
+    for ry, rx in relative:
+        down_to(1, ry, rx).start()
 
     most_pipe = pl.ds(0, PIPE - 1)
     pltpu.make_async_copy(score_in.at[most_pipe], score_in.at[most_pipe], score_sem.at[1]).wait()
@@ -348,67 +401,13 @@
 
     lax.fori_loop(1, PIPE, send_weights, 0)
 
-    loads[1].wait()
-    gate_up_pair.wait_recv()
-
-    def project(part, ry, rx):
-        first, count = PARTS[part]
-        which = chip_at(ry, rx)
-        start = pl.multiple_of(which * columns + first * LANES, LANES)
-        return jnp.dot(
-            gathered[part][which], gate_up[pl.ds(start, count * LANES), :],
-            preferred_element_type=jnp.float32,
-        )
-
-    both = project(0, 0, 0) + project(0, 1, 0)
-    take(1, 0, 3)
-    pass_on(1, (0, 3), plus, 0)
-    pass_on(1, (0, 3), up)
-    take(1, 0, 1)
-    pass_on(1, (0, 1), minus, 1)
-    pass_on(1, (0, 1), up)
-    for ry in range(NY):
-        both += project(0, ry, 3) + project(0, ry, 1)
-    for piece in range(2):
-        take(1, 0, 2, piece)
-        pass_on(1, (0, 2), up, piece)
-    for ry, rx in relative:
-        down_to(1, ry, rx).start()
-    both += project(1, 0, 0) + project(1, 0, 1) + project(1, 0, 2) + project(1, 0, 3)
-    for ry in range(NY):
-        for piece in range(2):
-            take(0, ry, 2, piece)
-        both += project(0, ry, 2)
-    for rx in (0, 3, 1):
-        take(1, 1, rx)
-        both += project(1, 1, rx)
-    for piece in range(2):
-        take(1, 1, 2, piece)
-    both += project(1, 1, 2)
-    parts = []
-    for k in range(CORES):
-        gate = both[:, 2 * k * units : (2 * k + 1) * units]
-        upper = both[:, (2 * k + 1) * units : (2 * k + 2) * units]
-        parts.append(gate / (1.0 + jnp.exp(-gate)) * upper)
-    hidden[chip] = jnp.concatenate(parts, axis=1).astype(jnp.bfloat16)
-
-    def hidden_to(ry, rx):
-        return remote(
-            hidden.at[chip], hidden.at[chip],
-            hidden_send.at[ry * NX + rx], hidden_recv.at[mirror[ry, rx]],
-            CORES * chip_at(ry, rx) + core, ep,
-        )
-
-    for ry, rx in relative:
-        hidden_to(ry, rx).start()
-
     down_pair(0).wait_recv()
     order = [(1, 0), (0, 1), (0, 3), (1, 1), (1, 3), (0, 2), (1, 2)]
 
     def lower(part, ry, rx):
         which = chip_at(ry, rx)
         return jnp.dot(
-            hidden[which], downs[part][which].reshape(CORES * units, PARTS[part][1] * LANES),
+            hidden[which], downs[part][which].reshape(CORES * units, DOWN_PARTS[part][1] * LANES),
             preferred_element_type=jnp.float32,
         )
 
@@ -481,7 +480,7 @@
         jnp.concatenate([chip_tokens[:, own:], padding], axis=1),
     )
 
-    rows_left(1)
+    rows_left(len(PARTS) - 1)
     pltpu.make_async_copy(
         score_out.at[most_pipe], score_out.at[most_pipe], score_sem.at[0]
     ).wait()
@@ -544,12 +543,13 @@
             pltpu.VMEM((tok, width), bf16),
             pltpu.VMEM((columns, experts), bf16),
             pltpu.VMEM((width, CORES * 2 * units), bf16),
-            pltpu.VMEM((CHIPS, CORES, units, PARTS[0][1] * LANES), bf16),
-            pltpu.VMEM((CHIPS, CORES, units, PARTS[1][1] * LANES), bf16),
-            pltpu.VMEM((2, NZ, PIECE, LANES), bf16),
-            pltpu.VMEM((2, NZ, PIECE, LANES), bf16),
-            pltpu.VMEM((CHIPS, half, PARTS[0][1] * LANES), bf16),
-            pltpu.VMEM((CHIPS, half, PARTS[1][1] * LANES), bf16),
+            *[
+                pltpu.VMEM((CHIPS, CORES, units, count * LANES), bf16)
+                for _, count in DOWN_PARTS
+            ],
+            pltpu.VMEM((len(PARTS), NZ, PIECE, LANES), bf16),
+            pltpu.VMEM((len(PARTS), NZ, PIECE, LANES), bf16),
+            *[pltpu.VMEM((CHIPS, half, count * LANES), bf16) for _, count in PARTS],
             pltpu.VMEM((CHIPS, half, CORES * units), bf16),
             pltpu.VMEM((CORES, NZ, 32, LANES), bf16),
             pltpu.VMEM((HALVES, NZ, 32, LANES), bf16),
@@ -557,8 +557,8 @@
             pltpu.VMEM((PIPE, group, experts), f32),
             pltpu.VMEM((group, 2 * half), f32),
             pltpu.VMEM((PIPE, group, 2 * half), f32),
-            dma((8,)), dma((4,)), dma((4,)),
-            dma((32,)), dma((4 * CHIPS,)), dma((6,)),
+            dma((8,)), dma((2 * len(PARTS),)), dma((2 * len(PARTS),)),
+            dma((9 * len(PARTS),)), dma((2 * len(PARTS) * CHIPS,)), dma((6,)),
             dma((2, 2 * CHIPS)), dma((CHIPS,)), dma((CHIPS,)),
             dma((2,)), dma((4,)), dma((2,)), dma((2,)),
         ],

time: 80.1 us -> 73.2 us (0.914)
  Pallas kernels: 78.3 us -> 71.4 us
    pallas_call x1, Pallas kernels: 78.3 us -> 71.4 us  [shards(): pl.pallas_call(kernel, out_shape=jax.ShapeDtypeStruct((width // PIPE, tok...]
where the time goes in v5:
time: 73.2 us; the launch traced here: 72.9 us
  Pallas kernels  71.4 us (98%)
  local copies, waits for them, and re-layouts  1.55 us (2%)
    pallas_call x1, Pallas kernels, shards(): pl.pallas_call(kernel, out_shape=jax.ShapeDtypeStruct((width // PIPE, tok...  71.4 us
    unnamed x1, local copies, waits for them, and re-layouts  1.55 us

profile of v5, /device:TPU:1, one launch (start us, length us, event | category | flops | bytes accessed | tf_op | source)
XLA Modules:
  0.0 72.9 jit_solution(17749828532078429925)
XLA Ops:
  0.0 71.4 %shard_map.64 = bf16[448,128]{1,0:T(8,128)(2,1)} custom-call(bf16[128,7168]{1,0:T(8,128)(2,1)} %tokens_hbm.1, f32[1,7168]{1,0:T(1,128)} %bitcast.4, bf16[448,256]{1,0:T(8,128)(2,1)} %router_hbm.1, s32[8,128]{1,0:T(8,128)} %bitcast.5, bf16[1,7168,128]{2,1,0:T(8,128)(2,1)} %gate_up_hbm.1, bf16[1,64,7168]{2,1,0:T(8,128)(2,1)} %down_hbm.1), custom_call_target="tpu_custom_call" | custom-call | flops 2000000000 | bytes 8000000 | tf_op jit(solution)/shard_map/pallas_call | solution.py:537
  71.4 1.6 %copy.8 = bf16[128,448]{0,1:T(8,128)(2,1)} copy(bf16[128,448]{0,1:T(8,128)(2,1)} %bitcast.3) | data formatting | bytes 229376

commit v6 on v5

--- a/solution.py
+++ b/solution.py
@@ -15,20 +15,21 @@
 NZ = 16
 HALVES = 2
 CAP = 8
-PARTS = ((0, 2), (2, 2), (4, 2), (6, 1))
-DOWN_PARTS = ((0, 4), (4, 3))
-PIECE = 16
+COLUMN_PARTS = ((0, 4), (4, 3))
+PARTS = tuple((rows, first, count) for rows in (0, 1) for first, count in COLUMN_PARTS)
+PIECE = 32
 Y_FIRST = (0, 2)
 ARRIVALS = (
     (0, 0, 0, None), (1, 0, 0, None), (0, 1, 0, None), (0, 0, 3, None), (0, 0, 1, None),
-    (2, 0, 0, None), (1, 0, 3, None), (1, 0, 1, None), (1, 1, 0, None), (0, 1, 3, None),
-    (0, 1, 1, None), (3, 0, 0, None), (0, 0, 2, 0), (0, 0, 2, 1), (2, 1, 0, None),
-    (2, 0, 3, None), (2, 0, 1, None), (1, 1, 3, None), (1, 0, 2, 0), (1, 0, 2, 1),
-    (0, 1, 2, 0), (0, 1, 2, 1), (1, 1, 1, None), (3, 0, 3, None), (3, 0, 1, None),
-    (3, 1, 0, None), (2, 1, 3, None), (2, 1, 1, None), (1, 1, 2, 0), (1, 1, 2, 1),
-    (2, 0, 2, 0), (2, 0, 2, 1), (3, 0, 2, 0), (3, 0, 2, 1), (3, 1, 3, None),
+    (2, 0, 0, None), (1, 0, 3, None), (1, 0, 1, None), (1, 1, 0, None), (3, 0, 0, None),
+    (0, 1, 3, None), (0, 1, 1, None), (2, 1, 0, None), (0, 0, 2, 0), (0, 0, 2, 1),
+    (1, 1, 3, None), (2, 0, 1, None), (1, 1, 1, None), (1, 0, 2, 0), (1, 0, 2, 1),
+    (2, 0, 3, None), (3, 1, 0, None), (3, 0, 3, None), (3, 0, 1, None), (1, 1, 2, 0),
+    (1, 1, 2, 1), (0, 1, 2, 0), (0, 1, 2, 1), (2, 1, 3, None), (2, 1, 1, None),
+    (2, 0, 2, 0), (2, 0, 2, 1), (3, 1, 3, None), (3, 0, 2, 0), (3, 0, 2, 1),
     (3, 1, 1, None), (2, 1, 2, 0), (2, 1, 2, 1), (3, 1, 2, 0), (3, 1, 2, 1),
 )
+DOWN_FROM, FIRST_HIDDEN, FIRST_RETURN = 3, 27, 34
 LANES = 128
 MESH = pl.DeviceIdType.MESH
 
@@ -88,6 +89,8 @@
     half = NZ * CAP
     own = columns // CORES
     units = down_a.shape[2]
+    parity = lax.rem(z, 2)
+    span = half // 2
     downs = (down_a, down_b)
     total_slots = HALVES * half
 
@@ -95,7 +98,7 @@
         return pl.ds(pl.multiple_of(which * columns, LANES), columns)
 
     def down_columns(part, which):
-        first, count = DOWN_PARTS[part]
+        first, count = COLUMN_PARTS[part]
         start = pl.multiple_of(which * columns + first * LANES, LANES)
         return down_hbm.at[0, :, pl.ds(start, count * LANES)]
 
@@ -172,7 +175,7 @@
         jnp.bfloat16
     )
     placed = jnp.dot(placing, normed, preferred_element_type=jnp.float32)
-    for part, (first, count) in enumerate(PARTS):
+    for part, (first, count) in enumerate(COLUMN_PARTS):
         pieces = [
             placed[:, at * LANES : (at + 1) * LANES].reshape(NZ, CAP, LANES)
             for at in range(first, first + count)
@@ -185,16 +188,16 @@
 
     def near_copy(part):
         return remote(
-            outbox.at[part, z], inbox.at[part, z],
-            near_sem.at[2 * part], near_sem.at[2 * part + 1], pipe, far_side * NZ + z,
+            outbox.at[part, z], inbox.at[parity, part, lax.div(z, 2)],
+            near_sem.at[part], near_sem.at[2 + part], pipe, far_side * NZ + z,
         )
 
     def send_rows(part):
         def dispatch(i, _):
             other = far_first(i)
             remote(
-                outbox.at[part, other], inbox.at[part, z],
-                out_sem.at[2 * part], out_sem.at[2 * part + 1],
+                outbox.at[part, other], inbox.at[parity, part, lax.div(z, 2)],
+                out_sem.at[part], out_sem.at[2 + 2 * parity + part],
                 pipe, far_side * NZ + other,
             ).start()
             return 0
@@ -208,12 +211,12 @@
         @pl.when(core == 0)
         def _():
             pltpu.make_async_copy(
-                outbox.at[part, z], inbox.at[part, z], near_sem.at[2 * part + 1]
+                outbox.at[part, z], inbox.at[parity, part, lax.div(z, 2)], near_sem.at[2 + part]
             ).start()
 
     def rows_left(part):
         pltpu.make_async_copy(
-            outbox.at[part, most], outbox.at[part, most], out_sem.at[2 * part]
+            outbox.at[part, most], outbox.at[part, most], out_sem.at[part]
         ).wait()
 
         @pl.when(core == 1)
@@ -221,7 +224,10 @@
             near_copy(part).wait_send()
 
     most = pl.ds(0, NZ - 1)
-    send_rows(0)
+
+    @pl.when(parity == 0)
+    def _():
+        send_rows(0)
 
     def chip_at(ry, rx):
         return lax.rem(y + ry, NY) * NX + lax.rem(x + rx, NX)
@@ -269,30 +275,42 @@
 
     lax.fori_loop(1, PIPE, send_scores, 0)
 
-    for part in range(1, len(PARTS) - 1):
-        rows_left(part - 1)
-        send_rows(part)
+    @pl.when(parity == 0)
+    def _():
+        rows_left(0)
+        send_rows(1)
 
     gathered = (rows_a, rows_b, rows_c, rows_d)
     sent = []
 
     def arrive(part):
-        first, count = PARTS[part]
-        pltpu.make_async_copy(
-            inbox.at[part, most], inbox.at[part, most], out_sem.at[2 * part + 1]
-        ).wait()
-        pltpu.make_async_copy(
-            inbox.at[part, 0], inbox.at[part, 0], near_sem.at[2 * part + 1]
-        ).wait()
-        arrived = inbox[part].astype(jnp.float32)
+        rows_half, _, count = PARTS[part]
+        column_part = part % 2
+        box = inbox.at[rows_half, column_part]
+        others = box.at[pl.ds(0, NZ // 2 - 1)]
+
+        @pl.when(parity == rows_half)
+        def _():
+            pltpu.make_async_copy(others, others, out_sem.at[2 + part]).wait()
+            pltpu.make_async_copy(box.at[0], box.at[0], near_sem.at[2 + column_part]).wait()
+
+        @pl.when(parity != rows_half)
+        def _():
+            pltpu.make_async_copy(box, box, out_sem.at[2 + part]).wait()
+            if rows_half == 0:
+                if column_part == 1:
+                    rows_left(0)
+                send_rows(column_part)
+
+        arrived = inbox[rows_half, column_part].astype(jnp.float32)
         for at in range(count):
             gathered[part][chip, :, at * LANES : (at + 1) * LANES] = (
-                arrived[:, at * CAP : (at + 1) * CAP, :].reshape(half, LANES).astype(jnp.bfloat16)
+                arrived[:, at * CAP : (at + 1) * CAP, :].reshape(span, LANES).astype(jnp.bfloat16)
             )
 
     def block_ref(part, ry, rx, piece):
         ref = gathered[part].at[chip_at(ry, rx)]
-        return ref if piece is None else ref.at[pl.ds(piece * (half // 2), half // 2), :]
+        return ref if piece is None else ref.at[pl.ds(piece * (span // 2), span // 2), :]
 
     def recv_sem(part, ry, rx, piece):
         return gather_recv.at[(part * CHIPS + (ry % NY) * NX + rx % NX) * 2 + (piece or 0)]
@@ -314,7 +332,7 @@
     up, plus, minus = (1, 0), (0, 1), (0, 3)
 
     def project(part, ry, rx):
-        first, count = PARTS[part]
+        _, first, count = PARTS[part]
         which = chip_at(ry, rx)
         start = pl.multiple_of(which * columns + first * LANES, LANES)
         return jnp.dot(
@@ -322,7 +340,77 @@
             preferred_element_type=jnp.float32,
         )
 
-    both = jnp.zeros((half, CORES * 2 * units), jnp.float32)
+    def hidden_to(rows_half, ry, rx):
+        ref = hidden.at[rows_half, chip]
+        return remote(
+            ref, ref, hidden_send.at[rows_half, ry * NX + rx],
+            hidden_recv.at[rows_half, mirror[ry, rx]],
+            CORES * chip_at(ry, rx) + core, ep,
+        )
+
+    def send_hidden(rows_half, both):
+        parts = []
+        for k in range(CORES):
+            gate = both[:, 2 * k * units : (2 * k + 1) * units]
+            upper = both[:, (2 * k + 1) * units : (2 * k + 2) * units]
+            parts.append(gate / (1.0 + jnp.exp(-gate)) * upper)
+        hidden[rows_half, chip] = jnp.concatenate(parts, axis=1).astype(jnp.bfloat16)
+        for ry, rx in relative:
+            hidden_to(rows_half, ry, rx).start()
+
+    order = [(1, 0), (0, 1), (0, 3), (1, 1), (1, 3), (0, 2), (1, 2)]
+
+    def lower(rows_half, part, ry, rx):
+        which = chip_at(ry, rx)
+        return jnp.dot(
+            hidden[rows_half, which],
+            downs[part][which].reshape(CORES * units, COLUMN_PARTS[part][1] * LANES),
+            preferred_element_type=jnp.float32,
+        )
+
+    def send_back(rows_half, j, result):
+        pieces = []
+        for at in range(4):
+            low, high = at * LANES, min((at + 1) * LANES, own)
+            piece = result[:, low:high]
+            if high - low < LANES:
+                piece = jnp.concatenate(
+                    [piece, jnp.zeros((span, LANES - (high - low)), jnp.float32)], axis=1
+                )
+            pieces.append(piece.reshape(NZ // 2, CAP, LANES))
+        back_out[rows_half, j] = jnp.concatenate(pieces, axis=1).astype(jnp.bfloat16)
+        apart = lax.rem(parity + rows_half, 2)
+
+        def send(steps):
+            other = lax.rem(z + 2 * steps + apart, NZ)
+            remote(
+                back_out.at[rows_half, j, lax.div(other, 2)], back_in.at[core, z],
+                back_sem.at[0], back_sem.at[1],
+                CORES * chip + j, far_side * NZ + other,
+            ).start()
+
+        def go(i, _):
+            send(NZ // 4 + lax.div(i, 2) * (1 - 2 * lax.rem(i, 2)))
+            return 0
+
+        lax.fori_loop(1, NZ // 2, go, 0)
+
+        @pl.when(apart == 1)
+        def _():
+            send(0)
+
+    def finish(rows_half):
+        low_part = lower(rows_half, 0, 0, 0)
+        for ry, rx in order:
+            hidden_to(rows_half, ry, (NX - rx) % NX).wait_recv()
+            low_part += lower(rows_half, 0, ry, rx)
+        send_back(rows_half, 0, low_part)
+        high_part = lower(rows_half, 1, 0, 0)
+        for ry, rx in order:
+            high_part += lower(rows_half, 1, ry, rx)
+        send_back(rows_half, 1, jnp.concatenate([low_part[:, own:], high_part], axis=1))
+
+    both = [jnp.zeros((span, CORES * 2 * units), jnp.float32) for _ in range(2)]
     for step, (part, ry, rx, piece) in enumerate(ARRIVALS):
         here = (ry, rx)
         if here == (0, 0):
@@ -345,32 +433,44 @@
             if part not in Y_FIRST and ry == 0 and rx != 2:
                 pass_on(part, here, up)
         if step == 0:
-            rows_left(len(PARTS) - 2)
-            send_rows(len(PARTS) - 1)
             loads[1].wait()
             gate_up_pair.wait_recv()
-        if (part, ry, rx) == (len(PARTS) - 1, 0, 0):
+        if DOWN_FROM <= step < DOWN_FROM + len(relative):
+            down_to(1, *relative[step - DOWN_FROM]).start()
+        if (part, ry, rx) == (2, 0, 0):
             share_down(0)
         if piece != 0:
-            both += project(part, ry, rx)
-    parts = []
-    for k in range(CORES):
-        gate = both[:, 2 * k * units : (2 * k + 1) * units]
-        upper = both[:, (2 * k + 1) * units : (2 * k + 2) * units]
-        parts.append(gate / (1.0 + jnp.exp(-gate)) * upper)
-    hidden[chip] = jnp.concatenate(parts, axis=1).astype(jnp.bfloat16)
-
-    def hidden_to(ry, rx):
-        return remote(
-            hidden.at[chip], hidden.at[chip],
-            hidden_send.at[ry * NX + rx], hidden_recv.at[mirror[ry, rx]],
-            CORES * chip_at(ry, rx) + core, ep,
-        )
-
-    for ry, rx in relative:
-        hidden_to(ry, rx).start()
-    for ry, rx in relative:
-        down_to(1, ry, rx).start()
+            both[part // 2] += project(part, ry, rx)
+        if step == FIRST_HIDDEN:
+            send_hidden(0, both[0])
+            share_down(1)
+        if step == FIRST_RETURN:
+            down_pair(0).wait_recv()
+            down_pair(1).wait_recv()
+            finish(0)
+    send_hidden(1, both[1])
+    finish(1)
+
+    back_near_out = back_out.at[parity]
+    back_zero = remote(
+        back_near_out.at[0, lax.div(z, 2)], back_in.at[core, z],
+        back_near.at[0], back_near.at[2 + core], CORES * chip, far_side * NZ + z,
+    )
+    back_one = remote(
+        back_near_out.at[1, lax.div(z, 2)], back_in.at[core, z],
+        back_near.at[1], back_near.at[2 + core], CORES * chip + 1, far_side * NZ + z,
+    )
+    back_one.start()
+
+    @pl.when(core == 1)
+    def _():
+        back_zero.start()
+
+    @pl.when(core == 0)
+    def _():
+        pltpu.make_async_copy(
+            back_near_out.at[0, lax.div(z, 2)], back_in.at[core, z], back_near.at[2 + core]
+        ).start()
 
     most_pipe = pl.ds(0, PIPE - 1)
     pltpu.make_async_copy(score_in.at[most_pipe], score_in.at[most_pipe], score_sem.at[1]).wait()
@@ -401,70 +501,6 @@
 
     lax.fori_loop(1, PIPE, send_weights, 0)
 
-    down_pair(0).wait_recv()
-    order = [(1, 0), (0, 1), (0, 3), (1, 1), (1, 3), (0, 2), (1, 2)]
-
-    def lower(part, ry, rx):
-        which = chip_at(ry, rx)
-        return jnp.dot(
-            hidden[which], downs[part][which].reshape(CORES * units, DOWN_PARTS[part][1] * LANES),
-            preferred_element_type=jnp.float32,
-        )
-
-    def go_back(j, result):
-        pieces = []
-        for at in range(4):
-            low, high = at * LANES, min((at + 1) * LANES, own)
-            piece = result[:, low:high]
-            if high - low < LANES:
-                piece = jnp.concatenate(
-                    [piece, jnp.zeros((half, LANES - (high - low)), jnp.float32)], axis=1
-                )
-            pieces.append(piece.reshape(NZ, CAP, LANES))
-        back_out[j] = jnp.concatenate(pieces, axis=1).astype(jnp.bfloat16)
-
-        def go(i, _):
-            other = far_first(i)
-            remote(
-                back_out.at[j, other], back_in.at[core, z], back_sem.at[0], back_sem.at[1],
-                CORES * chip + j, far_side * NZ + other,
-            ).start()
-            return 0
-
-        lax.fori_loop(1, NZ, go, 0)
-
-    low_part = lower(0, 0, 0)
-    for ry, rx in order:
-        hidden_to(ry, (NX - rx) % NX).wait_recv()
-        low_part += lower(0, ry, rx)
-    go_back(0, low_part)
-    back_zero = remote(
-        back_out.at[0, z], back_in.at[core, z], back_near.at[0], back_near.at[2 + core],
-        CORES * chip, far_side * NZ + z,
-    )
-
-    @pl.when(core == 1)
-    def _():
-        back_zero.start()
-
-    @pl.when(core == 0)
-    def _():
-        pltpu.make_async_copy(
-            back_out.at[0, z], back_in.at[core, z], back_near.at[2 + core]
-        ).start()
-
-    share_down(1)
-    down_pair(1).wait_recv()
-    high_part = lower(1, 0, 0)
-    for ry, rx in order:
-        high_part += lower(1, ry, rx)
-    go_back(1, jnp.concatenate([low_part[:, own:], high_part], axis=1))
-    back_one = remote(
-        back_out.at[1, z], back_in.at[core, z], back_near.at[1], back_near.at[2 + core],
-        CORES * chip + 1, far_side * NZ + z,
-    )
-    back_one.start()
-
     slots_all = slot_matrix(names, 0, total_slots)
     slots_now = jnp.where(
         side == 0, slots_all, jnp.concatenate([slots_all[half:], slots_all[:half]], axis=0)
@@ -480,7 +516,7 @@
         jnp.concatenate([chip_tokens[:, own:], padding], axis=1),
     )
 
-    rows_left(len(PARTS) - 1)
+    rows_left(1)
     pltpu.make_async_copy(
         score_out.at[most_pipe], score_out.at[most_pipe], score_sem.at[0]
     ).wait()
@@ -490,7 +526,8 @@
     for ry, rx in relative:
         down_to(0, ry, rx).wait_send()
         down_to(1, ry, rx).wait_send()
-        hidden_to(ry, rx).wait_send()
+        hidden_to(0, ry, rx).wait_send()
+        hidden_to(1, ry, rx).wait_send()
     for copy in sent:
         copy.wait_send()
     gate_up_pair.wait_send()
@@ -520,7 +557,7 @@
         back_zero.wait_send()
 
     back_one.wait_send()
-    pltpu.make_async_copy(back_out.at[:, most], back_out.at[:, most], back_sem.at[0]).wait()
+    pltpu.make_async_copy(back_in.at[:, most], back_in.at[:, most], back_sem.at[0]).wait()
 
 
 def shards(tokens, norm_gain, router, routes, w_gate_up, w_down):
@@ -545,21 +582,21 @@
             pltpu.VMEM((width, CORES * 2 * units), bf16),
             *[
                 pltpu.VMEM((CHIPS, CORES, units, count * LANES), bf16)
-                for _, count in DOWN_PARTS
+                for _, count in COLUMN_PARTS
             ],
-            pltpu.VMEM((len(PARTS), NZ, PIECE, LANES), bf16),
-            pltpu.VMEM((len(PARTS), NZ, PIECE, LANES), bf16),
-            *[pltpu.VMEM((CHIPS, half, count * LANES), bf16) for _, count in PARTS],
-            pltpu.VMEM((CHIPS, half, CORES * units), bf16),
-            pltpu.VMEM((CORES, NZ, 32, LANES), bf16),
+            pltpu.VMEM((len(COLUMN_PARTS), NZ, PIECE, LANES), bf16),
+            pltpu.VMEM((2, len(COLUMN_PARTS), NZ // 2, PIECE, LANES), bf16),
+            *[pltpu.VMEM((CHIPS, half // 2, count * LANES), bf16) for _, _, count in PARTS],
+            pltpu.VMEM((2, CHIPS, half // 2, CORES * units), bf16),
+            pltpu.VMEM((2, CORES, NZ // 2, 32, LANES), bf16),
             pltpu.VMEM((HALVES, NZ, 32, LANES), bf16),
             pltpu.VMEM((PIPE, group, experts), f32),
             pltpu.VMEM((PIPE, group, experts), f32),
             pltpu.VMEM((group, 2 * half), f32),
             pltpu.VMEM((PIPE, group, 2 * half), f32),
-            dma((8,)), dma((2 * len(PARTS),)), dma((2 * len(PARTS),)),
+            dma((8,)), dma((4,)), dma((6,)),
             dma((9 * len(PARTS),)), dma((2 * len(PARTS) * CHIPS,)), dma((6,)),
-            dma((2, 2 * CHIPS)), dma((CHIPS,)), dma((CHIPS,)),
+            dma((2, 2 * CHIPS)), dma((2, CHIPS)), dma((2, CHIPS)),
             dma((2,)), dma((4,)), dma((2,)), dma((2,)),
         ],
         compiler_params=pltpu.CompilerParams(

time: 73.2 us -> 71.2 us (0.973)
  the two profiles are of different devices: /device:TPU:1 before, /device:TPU:41 now
where the time goes in v6:
time: 71.2 us; the launch traced here: 70.9 us
  Pallas kernels  69.4 us (97%)
  local copies, waits for them, and re-layouts  1.55 us (2%)
    pallas_call x1, Pallas kernels, shards(): pl.pallas_call(kernel, out_shape=jax.ShapeDtypeStruct((width // PIPE, tok...  69.4 us
    unnamed x1, local copies, waits for them, and re-layouts  1.55 us

profile of v6, /device:TPU:41, one launch (start us, length us, event | category | flops | bytes accessed | tf_op | source)
XLA Modules:
  0.0 70.9 jit_solution(7746427749502527108)
XLA Ops:
  0.0 69.4 %shard_map.64 = bf16[448,128]{1,0:T(8,128)(2,1)} custom-call(bf16[128,7168]{1,0:T(8,128)(2,1)} %tokens_hbm.1, f32[1,7168]{1,0:T(1,128)} %bitcast.4, bf16[448,256]{1,0:T(8,128)(2,1)} %router_hbm.1, s32[8,128]{1,0:T(8,128)} %bitcast.5, bf16[1,7168,128]{2,1,0:T(8,128)(2,1)} %gate_up_hbm.1, bf16[1,64,7168]{2,1,0:T(8,128)(2,1)} %down_hbm.1), custom_call_target="tpu_custom_call" | custom-call | flops 2000000000 | bytes 8000000 | tf_op jit(solution)/shard_map/pallas_call | solution.py:574
  69.4 1.6 %copy.8 = bf16[128,448]{0,1:T(8,128)(2,1)} copy(bf16[128,448]{0,1:T(8,128)(2,1)} %bitcast.3) | data formatting | bytes 229376

commit v7 on v6

--- a/solution.py
+++ b/solution.py
@@ -18,20 +18,28 @@
 COLUMN_PARTS = ((0, 4), (4, 3))
 PARTS = tuple((rows, first, count) for rows in (0, 1) for first, count in COLUMN_PARTS)
 PIECE = 32
-Y_FIRST = (0, 2)
+Y_FIRST = (1, 2)
 ARRIVALS = (
-    (0, 0, 0, None), (1, 0, 0, None), (0, 1, 0, None), (0, 0, 3, None), (0, 0, 1, None),
-    (2, 0, 0, None), (1, 0, 3, None), (1, 0, 1, None), (1, 1, 0, None), (3, 0, 0, None),
-    (0, 1, 3, None), (0, 1, 1, None), (2, 1, 0, None), (0, 0, 2, 0), (0, 0, 2, 1),
-    (1, 1, 3, None), (2, 0, 1, None), (1, 1, 1, None), (1, 0, 2, 0), (1, 0, 2, 1),
-    (2, 0, 3, None), (3, 1, 0, None), (3, 0, 3, None), (3, 0, 1, None), (1, 1, 2, 0),
-    (1, 1, 2, 1), (0, 1, 2, 0), (0, 1, 2, 1), (2, 1, 3, None), (2, 1, 1, None),
-    (2, 0, 2, 0), (2, 0, 2, 1), (3, 1, 3, None), (3, 0, 2, 0), (3, 0, 2, 1),
-    (3, 1, 1, None), (2, 1, 2, 0), (2, 1, 2, 1), (3, 1, 2, 0), (3, 1, 2, 1),
+    (0, 0, 0, None), (1, 0, 0, None), (0, 0, 3, None), (0, 0, 1, None), (0, 1, 0, None),
+    (2, 0, 0, None), (1, 0, 3, None), (1, 0, 1, None), (1, 1, 0, None), (0, 0, 2, 0),
+    (0, 0, 2, 1), (0, 1, 3, None), (3, 0, 0, None), (2, 0, 3, None), (2, 0, 1, None),
+    (1, 0, 2, 0), (1, 0, 2, 1), (0, 1, 1, None), (1, 1, 3, None), (1, 1, 1, None),
+    (2, 1, 0, None), (3, 0, 1, None), (0, 1, 2, 0), (2, 0, 2, 1), (0, 1, 2, 1),
+    (3, 0, 3, None), (2, 0, 2, 0), (1, 1, 2, 0), (1, 1, 2, 1), (3, 1, 0, None),
+    (2, 1, 3, None), (2, 1, 1, None), (3, 0, 2, 1), (3, 0, 2, 0), (2, 1, 2, 0),
+    (2, 1, 2, 1), (3, 1, 1, None), (3, 1, 3, None), (3, 1, 2, 1), (3, 1, 2, 0),
 )
-DOWN_FROM, FIRST_HIDDEN, FIRST_RETURN = 3, 27, 34
+DOWN_FROM, FIRST_HIDDEN, FIRST_RETURN = 9, 28, 33
 LANES = 128
 MESH = pl.DeviceIdType.MESH
+
+
+def mod(value, size):
+    return value & (size - 1)
+
+
+def quotient(value, size):
+    return value >> (size.bit_length() - 1)
 
 
 def remote(src, dst, send, recv, pipe, ep):
@@ -78,10 +86,10 @@
     score_sem, weight_sem,
 ):
     pipe, ep = lax.axis_index("pipe"), lax.axis_index("ep")
-    core, chip = lax.rem(pipe, CORES), lax.div(pipe, CORES)
-    x, y = lax.rem(chip, NX), lax.div(chip, NX)
-    z, side = lax.rem(ep, NZ), lax.div(ep, NZ)
-    far_side = lax.rem(side + core, HALVES)
+    core, chip = mod(pipe, CORES), quotient(pipe, CORES)
+    x, y = mod(chip, NX), quotient(chip, NX)
+    z, side = mod(ep, NZ), quotient(ep, NZ)
+    far_side = mod(side + core, HALVES)
     partner = pipe + 1 - 2 * core
     tok, width = tokens.shape
     columns = width // CHIPS
@@ -89,7 +97,7 @@
     half = NZ * CAP
     own = columns // CORES
     units = down_a.shape[2]
-    parity = lax.rem(z, 2)
+    parity = mod(z, 2)
     span = half // 2
     downs = (down_a, down_b)
     total_slots = HALVES * half
@@ -103,7 +111,7 @@
         return down_hbm.at[0, :, pl.ds(start, count * LANES)]
 
     def far_first(i):
-        return lax.rem(z + NZ // 2 + lax.div(i, 2) * (1 - 2 * lax.rem(i, 2)), NZ)
+        return mod(z + NZ // 2 + quotient(i, 2) * (1 - 2 * mod(i, 2)), NZ)
 
     own_lanes = pl.ds(pl.multiple_of(core * 2 * units, LANES), 2 * units)
     quarter = width // 4
@@ -122,18 +130,18 @@
 
     def greet_pipe(i, _):
         pl.semaphore_signal(
-            barrier, inc=1, device_id=(lax.rem(pipe + i, PIPE), ep), device_id_type=MESH
+            barrier, inc=1, device_id=(mod(pipe + i, PIPE), ep), device_id_type=MESH
         )
         return 0
 
     lax.fori_loop(1, PIPE, greet_pipe, 0)
 
     def greet_ep(i, _):
-        other = lax.rem(z + i, NZ)
+        other = mod(z + i, NZ)
         for k in range(CORES):
             pl.semaphore_signal(
                 barrier, inc=1,
-                device_id=(CORES * chip + k, lax.rem(side + k, HALVES) * NZ + other),
+                device_id=(CORES * chip + k, mod(side + k, HALVES) * NZ + other),
                 device_id_type=MESH,
             )
         return 0
@@ -149,7 +157,7 @@
         pl.semaphore_signal(barrier, inc=1, device_id=(partner, ep), device_id_type=MESH)
 
     names = routes_ref[...]
-    placing = slot_matrix(names, lax.rem(core + side, HALVES) * NZ, half).astype(jnp.bfloat16)
+    placing = slot_matrix(names, mod(core + side, HALVES) * NZ, half).astype(jnp.bfloat16)
 
     squares = jnp.zeros((tok, LANES), jnp.float32)
     for n in range(4):
@@ -188,21 +196,18 @@
 
     def near_copy(part):
         return remote(
-            outbox.at[part, z], inbox.at[parity, part, lax.div(z, 2)],
+            outbox.at[part, z], inbox.at[parity, part, quotient(z, 2)],
             near_sem.at[part], near_sem.at[2 + part], pipe, far_side * NZ + z,
         )
 
     def send_rows(part):
-        def dispatch(i, _):
+        for i in range(1, NZ):
             other = far_first(i)
             remote(
-                outbox.at[part, other], inbox.at[parity, part, lax.div(z, 2)],
+                outbox.at[part, other], inbox.at[parity, part, quotient(z, 2)],
                 out_sem.at[part], out_sem.at[2 + 2 * parity + part],
                 pipe, far_side * NZ + other,
             ).start()
-            return 0
-
-        lax.fori_loop(1, NZ, dispatch, 0)
 
         @pl.when(core == 1)
         def _():
@@ -211,7 +216,7 @@
         @pl.when(core == 0)
         def _():
             pltpu.make_async_copy(
-                outbox.at[part, z], inbox.at[parity, part, lax.div(z, 2)], near_sem.at[2 + part]
+                outbox.at[part, z], inbox.at[parity, part, quotient(z, 2)], near_sem.at[2 + part]
             ).start()
 
     def rows_left(part):
@@ -230,7 +235,7 @@
         send_rows(0)
 
     def chip_at(ry, rx):
-        return lax.rem(y + ry, NY) * NX + lax.rem(x + rx, NX)
+        return mod(y + ry, NY) * NX + mod(x + rx, NX)
 
     relative = [(ry, rx) for rx in (2, 1, 3, 0) for ry in (1, 0) if (ry, rx) != (0, 0)]
     mirror = {(ry, rx): ry * NX + (NX - rx) % NX for ry, rx in relative}
@@ -267,7 +272,7 @@
     score_in[pipe] = score_out[pipe]
 
     def send_scores(i, _):
-        other = lax.rem(pipe + i, PIPE)
+        other = mod(pipe + i, PIPE)
         remote(
             score_out.at[other], score_in.at[pipe], score_sem.at[0], score_sem.at[1], other, ep
         ).start()
@@ -379,21 +384,18 @@
                 )
             pieces.append(piece.reshape(NZ // 2, CAP, LANES))
         back_out[rows_half, j] = jnp.concatenate(pieces, axis=1).astype(jnp.bfloat16)
-        apart = lax.rem(parity + rows_half, 2)
+        apart = mod(parity + rows_half, 2)
 
         def send(steps):
-            other = lax.rem(z + 2 * steps + apart, NZ)
+            other = mod(z + 2 * steps + apart, NZ)
             remote(
-                back_out.at[rows_half, j, lax.div(other, 2)], back_in.at[core, z],
+                back_out.at[rows_half, j, quotient(other, 2)], back_in.at[core, z],
                 back_sem.at[0], back_sem.at[1],
                 CORES * chip + j, far_side * NZ + other,
             ).start()
 
-        def go(i, _):
-            send(NZ // 4 + lax.div(i, 2) * (1 - 2 * lax.rem(i, 2)))
-            return 0
-
-        lax.fori_loop(1, NZ // 2, go, 0)
+        for i in range(1, NZ // 2):
+            send(NZ // 4 + quotient(i, 2) * (1 - 2 * mod(i, 2)))
 
         @pl.when(apart == 1)
         def _():
@@ -411,6 +413,7 @@
         send_back(rows_half, 1, jnp.concatenate([low_part[:, own:], high_part], axis=1))
 
     both = [jnp.zeros((span, CORES * 2 * units), jnp.float32) for _ in range(2)]
+    seen = set()
     for step, (part, ry, rx, piece) in enumerate(ARRIVALS):
         here = (ry, rx)
         if here == (0, 0):
@@ -439,7 +442,8 @@
             down_to(1, *relative[step - DOWN_FROM]).start()
         if (part, ry, rx) == (2, 0, 0):
             share_down(0)
-        if piece != 0:
+        seen.add((part, ry, rx, piece))
+        if piece is None or (part, ry, rx, 1 - piece) in seen:
             both[part // 2] += project(part, ry, rx)
         if step == FIRST_HIDDEN:
             send_hidden(0, both[0])
@@ -453,11 +457,11 @@
 
     back_near_out = back_out.at[parity]
     back_zero = remote(
-        back_near_out.at[0, lax.div(z, 2)], back_in.at[core, z],
+        back_near_out.at[0, quotient(z, 2)], back_in.at[core, z],
         back_near.at[0], back_near.at[2 + core], CORES * chip, far_side * NZ + z,
     )
     back_one = remote(
-        back_near_out.at[1, lax.div(z, 2)], back_in.at[core, z],
+        back_near_out.at[1, quotient(z, 2)], back_in.at[core, z],
         back_near.at[1], back_near.at[2 + core], CORES * chip + 1, far_side * NZ + z,
     )
     back_one.start()
@@ -469,7 +473,7 @@
     @pl.when(core == 0)
     def _():
         pltpu.make_async_copy(
-            back_near_out.at[0, lax.div(z, 2)], back_in.at[core, z], back_near.at[2 + core]
+            back_near_out.at[0, quotient(z, 2)], back_in.at[core, z], back_near.at[2 + core]
         ).start()
 
     most_pipe = pl.ds(0, PIPE - 1)
@@ -487,7 +491,7 @@
     fraction = 2.5 * affinity / jnp.sum(chosen * affinity, axis=1, keepdims=True)
     spread_row = lax.broadcasted_iota(jnp.int32, (experts, total_slots), 0)
     spread_lane = lax.broadcasted_iota(jnp.int32, (experts, total_slots), 1)
-    slot_expert = lax.rem(spread_lane // CAP + side * NZ, HALVES * NZ)
+    slot_expert = mod(spread_lane // CAP + side * NZ, HALVES * NZ)
     weight_out[...] = jnp.dot(
         fraction, jnp.where(spread_row == slot_expert, 1.0, 0.0),
         preferred_element_type=jnp.float32, precision=lax.Precision.HIGHEST,
@@ -495,7 +499,7 @@
     weight_in[pipe] = weight_out[...]
 
     def send_weights(i, _):
-        other = lax.rem(pipe + i, PIPE)
+        other = mod(pipe + i, PIPE)
         remote(weight_out, weight_in.at[pipe], weight_sem.at[0], weight_sem.at[1], other, ep).start()
         return 0
 

time: 71.2 us -> 69.4 us (0.975)
  the two profiles are of different devices: /device:TPU:41 before, /device:TPU:49 now
where the time goes in v7:
time: 69.4 us; the launch traced here: 69.2 us
  Pallas kernels  67.6 us (97%)
  local copies, waits for them, and re-layouts  1.55 us (2%)
    pallas_call x1, Pallas kernels, shards(): pl.pallas_call(kernel, out_shape=jax.ShapeDtypeStruct((width // PIPE, tok...  67.6 us
    unnamed x1, local copies, waits for them, and re-layouts  1.55 us

profile of v7, /device:TPU:49, one launch (start us, length us, event | category | flops | bytes accessed | tf_op | source)
XLA Modules:
  0.0 69.2 jit_solution(6722257497152549993)
XLA Ops:
  0.0 67.6 %shard_map.64 = bf16[448,128]{1,0:T(8,128)(2,1)} custom-call(bf16[128,7168]{1,0:T(8,128)(2,1)} %tokens_hbm.1, f32[1,7168]{1,0:T(1,128)} %bitcast.4, bf16[448,256]{1,0:T(8,128)(2,1)} %router_hbm.1, s32[8,128]{1,0:T(8,128)} %bitcast.5, bf16[1,7168,128]{2,1,0:T(8,128)(2,1)} %gate_up_hbm.1, bf16[1,64,7168]{2,1,0:T(8,128)(2,1)} %down_hbm.1), custom_call_target="tpu_custom_call" | custom-call | flops 2000000000 | bytes 8000000 | tf_op jit(solution)/shard_map/pallas_call | solution.py:578
  67.6 1.6 %copy.8 = bf16[128,448]{0,1:T(8,128)(2,1)} copy(bf16[128,448]{0,1:T(8,128)(2,1)} %bitcast.3) | data formatting | bytes 229376

commit v8 on v7

--- a/solution.py
+++ b/solution.py
@@ -128,16 +128,8 @@
 
     barrier = pltpu.get_barrier_semaphore()
 
-    def greet_pipe(i, _):
-        pl.semaphore_signal(
-            barrier, inc=1, device_id=(mod(pipe + i, PIPE), ep), device_id_type=MESH
-        )
-        return 0
-
-    lax.fori_loop(1, PIPE, greet_pipe, 0)
-
     def greet_ep(i, _):
-        other = mod(z + i, NZ)
+        other = far_first(i)
         for k in range(CORES):
             pl.semaphore_signal(
                 barrier, inc=1,
@@ -155,6 +147,14 @@
     @pl.when(core == 1)
     def _():
         pl.semaphore_signal(barrier, inc=1, device_id=(partner, ep), device_id_type=MESH)
+
+    def greet_pipe(i, _):
+        pl.semaphore_signal(
+            barrier, inc=1, device_id=(mod(pipe + i, PIPE), ep), device_id_type=MESH
+        )
+        return 0
+
+    lax.fori_loop(1, PIPE, greet_pipe, 0)
 
     names = routes_ref[...]
     placing = slot_matrix(names, mod(core + side, HALVES) * NZ, half).astype(jnp.bfloat16)

time: 69.4 us -> 71.5 us (1.030)
  the two profiles are of different devices: /device:TPU:49 before, /device:TPU:35 now
where the time goes in v8:
time: 71.5 us; the launch traced here: 71.3 us
  Pallas kernels  69.7 us (97%)
  local copies, waits for them, and re-layouts  1.55 us (2%)
    pallas_call x1, Pallas kernels, shards(): pl.pallas_call(kernel, out_shape=jax.ShapeDtypeStruct((width // PIPE, tok...  69.7 us
    unnamed x1, local copies, waits for them, and re-layouts  1.55 us

profile of v8, /device:TPU:35, one launch (start us, length us, event | category | flops | bytes accessed | tf_op | source)
XLA Modules:
  0.0 71.3 jit_solution(8848687158544494569)
XLA Ops:
  0.0 69.7 %shard_map.64 = bf16[448,128]{1,0:T(8,128)(2,1)} custom-call(bf16[128,7168]{1,0:T(8,128)(2,1)} %tokens_hbm.1, f32[1,7168]{1,0:T(1,128)} %bitcast.4, bf16[448,256]{1,0:T(8,128)(2,1)} %router_hbm.1, s32[8,128]{1,0:T(8,128)} %bitcast.5, bf16[1,7168,128]{2,1,0:T(8,128)(2,1)} %gate_up_hbm.1, bf16[1,64,7168]{2,1,0:T(8,128)(2,1)} %down_hbm.1), custom_call_target="tpu_custom_call" | custom-call | flops 2000000000 | bytes 8000000 | tf_op jit(solution)/shard_map/pallas_call | solution.py:578
  69.8 1.6 %copy.8 = bf16[128,448]{0,1:T(8,128)(2,1)} copy(bf16[128,448]{0,1:T(8,128)(2,1)} %bitcast.3) | data formatting | bytes 229376
